TPU v7x, 128 devices: a whole 4x4x4 slice. The times are simulated.
128 devices in a mesh: sn: 32 (over x, y, core), blk: 4 (over z).
Axes of the slice: x: 4, y: 4, z: 4, core: 2. Of those that a mesh axis runs over, the one named last changes fastest.
Arguments:
- root_inverse: float32 [8192, 8192], P('sn'), as said below
- structure: int32 [32, 4], replicated, may hold values from 0 to 31, as said below
- panel_one: float32 [32, 1024, 256], P('sn', 'blk'), may hold values from -0.375 to 0.375
- inverse_one: float32 [32, 256, 256], P('sn'), as said below
- parent_two: float32 [32, 256, 256], P('sn'), may hold values from -0.375 to 0.375
- panel_two: float32 [32, 1024, 256], P('sn', 'blk'), may hold values from -0.375 to 0.375
- inverse_two: float32 [32, 256, 256], P('sn'), as said below
Outputs:
- sigma_diag_one: float32 [32, 256, 256], P('sn')
- sigma_off_one: float32 [32, 1024, 256], P('sn', 'blk')
- sigma_diag_two: float32 [32, 256, 256], P('sn')
- sigma_par_two: float32 [32, 256, 256], P('sn')
- sigma_root_two: float32 [32, 1024, 256], P('sn', 'blk')
Inputs may be any that keep to these rules, and one draw needn't show every extreme that they name: `structure`: each row holds 4 distinct block indices. `inverse_one`: lower triangular; diagonal between 0.5 and 1.5. `inverse_two`: lower triangular; diagonal between 0.5 and 1.5. `root_inverse`: Symmetric.
All inputs are finite; a program needn't handle non-finite values.
Results may differ from a plain program's by a relative error of at most 0.00011.
Values sent between devices are 32-bit elements; how exact they have to be, the bound alone decides.
A program may use at most 128 MiB of HBM per device.

v0:
```python
import jax
import jax.numpy as jnp
from jax import lax
from jax.sharding import PartitionSpec as P


def product(left, right):
    return jnp.dot(left, right, precision=lax.Precision.HIGHEST, preferred_element_type=jnp.float32)


def per_device(root_inverse, structure, panel_one, inverse_one, parent_two, panel_two, inverse_two):
    width = inverse_one.shape[-1]
    groups = lax.axis_size("blk")
    per_group = structure.shape[1] // groups
    owner = lax.axis_index("sn")
    position_group = lax.axis_index("blk")
    inv_one = inverse_one[0]
    inv_two = inverse_two[0]
    u_one = product(panel_one[0], inv_one)
    u_root = product(panel_two[0], inv_two)
    u_par = product(parent_two[0], inv_two)
    stacked = jnp.concatenate([u_one, u_root], axis=1)
    group_lists = lax.dynamic_slice_in_dim(structure, position_group * per_group, per_group, 1)
    block_count = root_inverse.shape[1] // width
    local_rows = root_inverse.reshape(root_inverse.shape[0], block_count, width)
    own_list = lax.dynamic_index_in_dim(structure, owner, 0, keepdims=False)
    piece = lax.all_gather(stacked[None], "sn", axis=0, tiled=True)
    count = piece.shape[0]
    chosen = jnp.take(local_rows, group_lists, axis=1)
    panels = piece.reshape(count, per_group, width, 2 * width)
    terms = jnp.einsum(
        "rnkc,nkcd->nrd",
        chosen,
        panels,
        precision=lax.Precision.HIGHEST,
        preferred_element_type=jnp.float32,
    )
    reduced = lax.psum_scatter(terms, "blk", scatter_dimension=1, tiled=True)
    arrived = lax.all_to_all(reduced, "sn", split_axis=0, concat_axis=0, tiled=True)
    selected = jnp.take(arrived, own_list, axis=0)
    combined = lax.all_to_all(selected, "blk", split_axis=0, concat_axis=1, tiled=True)
    combined = combined.reshape(per_group * width, 2 * width)
    w_one = combined[:, :width]
    w_two = combined[:, width:]
    off_one = -w_one
    square_one = product(inv_one.T, inv_one)
    square_two = product(inv_two.T, inv_two)
    diag_term = product(u_one.T, w_one)
    root_two = -(w_two + product(off_one, u_par))
    child_term = product(u_root.T, root_two)
    diag_one = square_one + lax.psum(diag_term, "blk")
    parent_total, child_total = lax.psum((product(off_one.T, u_root), child_term), "blk")
    par_two = -(parent_total + product(diag_one, u_par))
    diag_two = square_two - product(u_par.T, par_two) - child_total
    return (diag_one[None], off_one[None], diag_two[None], par_two[None], root_two[None])


def solution(mesh):
    return jax.shard_map(
        per_device,
        mesh=mesh,
        in_specs=(
            P("sn", None),
            P(),
            P("sn", "blk", None),
            P("sn", None, None),
            P("sn", None, None),
            P("sn", "blk", None),
            P("sn", None, None),
        ),
        out_specs=(
            P("sn", None, None),
            P("sn", "blk", None),
            P("sn", None, None),
            P("sn", None, None),
            P("sn", "blk", None),
        ),
        check_vma=False,
    )
```

profile of v0, /device:TPU:0, one launch (start us, length us, event | category | flops | bytes accessed | tf_op | source)
XLA Modules:
  0.0 421.3 jit_solution(6829219561005356829)
XLA Ops:
  7.2 0.0 copy-start
  7.2 0.0 all-gather.3.cloned.1.call-start
  7.2 0.9 copy-done
  8.1 1.5 fusion.14
  9.7 1.6 fusion.17
  11.3 0.8 pad_maximum_fusion
  12.1 0.0 all-gather.3.cloned.1.call-update
  12.2 0.0 reduce-scatter.2.cloned.1.call-start
  12.2 9.0 %copy.14 = f32[256,8192]{0,1:T(8,128)} copy(f32[256,8192]{1,0:T(8,128)} %param.7) | data formatting | bytes 16777216 | tf_op args[0]
  21.2 0.0 copy-start.6
  21.2 9.1 %copy.15 = f32[256,32,256]{2,0,1:T(8,128)} copy(f32[256,32,256]{0,2,1:T(8,128)} %bitcast.52) | data formatting | bytes 16777216 | tf_op jit(solution)/shard_map/reshape | solution.py:25
  30.3 0.0 copy-done.6
  30.3 7.8 %gather_fusion = f32[32,256,256]{2,1,0:T(8,128)} fusion(f32[256,32,256]{2,0,1:T(8,128)} %copy.15, s32[1024]{0:T(1024)S(1)} %pad_clamp_fusion.1), kind=kCustom, calls=%fused_computation | custom fusion | bytes 16777344 | tf_op jit(solution)/shard_map/jit(_take)/gather | solution.py:29
  38.1 57.6 %all-gather.3.cloned.1.call-done = f32[8192,512]{0,1:T(8,128)} async-done(((f32[256,512]{0,1:T(8,128)}), f32[8192,512]{0,1:T(8,128)}) %all-gather.3.cloned.1.call-update) | async-done | bytes 16777232 | tf_op jit(solution)/shard_map/all_gather | solution.py:27
  95.7 17.5 %copy.17 = f32[8192,512]{1,0:T(8,128)} copy(f32[8192,512]{0,1:T(8,128)} %all-gather.3.cloned.1.call-done) | data formatting | bytes 33554432 | tf_op jit(solution)/shard_map/all_gather | solution.py:27
  113.2 23.5 %fusion = f32[32,256,512]{2,1,0:T(8,128)} fusion(f32[32,256,512]{2,1,0:T(8,128)} %bitcast.51, f32[32,256,256]{2,1,0:T(8,128)} %gather_fusion, pred[32]{0:T(512)(128)(4,1)S(1)} %get-tuple-element.8), kind=kOutput, calls=%fused_computation.2 | convolution fusion | flops 12886999040 | bytes 41943072 | tf_op jit(solution)/shard_map/rnkc,nkcd->nrd/dot_general | solution.py:31
  136.6 0.0 reduce-scatter.2.cloned.1.call-update
  136.7 0.0 copy-start.5
  136.7 0.0 copy-start.1
  136.7 148.4 %reduce-scatter.2.cloned.1.call-done = f32[32,64,512]{2,1,0:T(8,128)} async-done(((f32[32,256,512]{2,1,0:T(8,128)}), f32[32,64,512]{2,1,0:T(8,128)}) %reduce-scatter.2.cloned.1.call-update) | async-done | bytes 4194320 | tf_op jit(solution)/shard_map/reduce_scatter | solution.py:38
  285.1 7.2 %all-to-all-start = ((f32[32,64,512]{2,1,0:T(8,128)}), f32[32,64,512]{2,1,0:T(8,128)}, u32[]{:S(2)}, u32[]{:S(2)}) async-start(f32[32,64,512]{2,1,0:T(8,128)} %reduce-scatter.2.cloned.1.call-done), calls=%async_computation.1 | async-start | bytes 8388608 | tf_op jit(solution)/shard_map/all_to_all | solution.py:39
  292.4 0.2 dynamic-slice_reduce_fusion
  292.6 52.6 %all-to-all-done = f32[32,64,512]{2,1,0:T(8,128)} async-done(((f32[32,64,512]{2,1,0:T(8,128)}), f32[32,64,512]{2,1,0:T(8,128)}, u32[]{:S(2)}, u32[]{:S(2)}) %all-to-all-start) | async-done | bytes 4194336 | tf_op jit(solution)/shard_map/all_to_all | solution.py:39
  345.1 2.8 gather_fusion.1
  347.9 0.9 broadcast_select_fusion
  348.8 3.5 all-to-all-start.1
  352.3 0.2 all-reduce.3.cloned.1.call-start
  352.5 0.0 copy-done.5
  352.6 0.4 fusion.9
  352.9 8.9 %all-to-all-done.1 = f32[4,64,512]{2,1,0:T(8,128)S(1)} async-done(((f32[4,64,512]{2,1,0:T(8,128)}), f32[4,64,512]{2,1,0:T(8,128)S(1)}, u32[]{:S(2)}, u32[]{:S(2)}) %all-to-all-start.1) | async-done | bytes 524320 | tf_op jit(solution)/shard_map/all_to_all | solution.py:41
  361.8 1.3 fusion.23
  363.1 1.1 fusion.21
  364.2 0.4 fusion.5
  364.6 0.0 copy-start.2
  364.6 1.1 fusion.27
  365.7 0.0 all-reduce.3.cloned.1.call-update
  365.7 0.6 fusion.12
  366.3 0.7 fusion.24
  367.1 42.3 %all-reduce.3.cloned.1.call-done = (f32[256,256]{1,0:T(8,128)}, f32[256,256]{1,0:T(8,128)}, f32[256,256]{1,0:T(8,128)}) async-done(((f32[256,256]{1,0:T(8,128)}, f32[256,256]{1,0:T(8,128)}, f32[256,256]{1,0:T(8,128)}), (f32[256,256]{1,0:T(8,128)}, f32[256,256]{1,0:T(8,128)}, f32[256,256]{1,0:T(8,128)})) %all-reduce.3.cloned.1.call-update) | async-done | bytes 786448 | tf_op jit(solution)/shard_map/psum | solution.py:51
  409.4 0.0 copy-done.1
  409.4 1.5 convolution_add_fusion.2
  410.9 0.0 copy-start.3
  410.9 1.4 fusion.8
  412.4 0.0 copy-start.4
  412.4 2.4 fusion.7
  414.7 0.0 copy-done.2
  414.7 0.0 copy-done.3
  414.7 0.0 copy-done.4
  (5 shorter events, 0.0 us)
Async XLA Ops:
  7.2 1.0 copy-start
  7.2 88.5 %all-gather.3.cloned.1.call-start = ((), (), s32[]{:S(2)}) async-start(), calls=%async_computation.4 | async-start | bytes 17301504 | tf_op jit(solution)/shard_map/all_gather | solution.py:27
  12.2 273.0 %reduce-scatter.2.cloned.1.call-start = ((), (), s32[]{:S(2)}) async-start(), calls=%async_computation.3 | async-start | bytes 20971520 | tf_op jit(solution)/shard_map/reduce_scatter | solution.py:38
  21.2 9.1 %copy-start.6 = (s32[32,4]{0,1:T(4,128)S(1)}, s32[32,4]{0,1:T(4,128)}, u32[]{:S(2)}) copy-start(s32[32,4]{0,1:T(4,128)} %param.8) | copy-start | bytes 1540
  136.7 215.9 %copy-start.5 = (f32[1,256,256]{2,1,0:T(8,128)S(1)}, f32[1,256,256]{2,1,0:T(8,128)}, u32[]{:S(2)}) copy-start(f32[1,256,256]{2,1,0:T(8,128)} %param.11) | copy-start | bytes 786436
  136.7 272.7 %copy-start.1 = (f32[1,256,256]{2,1,0:T(8,128)S(1)}, f32[1,256,256]{2,1,0:T(8,128)}, u32[]{:S(2)}) copy-start(f32[1,256,256]{2,1,0:T(8,128)} %param.10) | copy-start | bytes 786436
  285.1 60.0 %all-to-all-start = ((f32[32,64,512]{2,1,0:T(8,128)}), f32[32,64,512]{2,1,0:T(8,128)}, u32[]{:S(2)}, u32[]{:S(2)}) async-start(f32[32,64,512]{2,1,0:T(8,128)} %reduce-scatter.2.cloned.1.call-done), calls=%async_computation.1 | async-start | bytes 8388608 | tf_op jit(solution)/shard_map/all_to_all | solution.py:39
  348.8 13.0 %all-to-all-start.1 = ((f32[4,64,512]{2,1,0:T(8,128)}), f32[4,64,512]{2,1,0:T(8,128)S(1)}, u32[]{:S(2)}, u32[]{:S(2)}) async-start(f32[4,64,512]{2,1,0:T(8,128)} %broadcast_select_fusion), calls=%async_computation.2 | async-start | bytes 1048576 | tf_op jit(solution)/shard_map/all_to_all | solution.py:41
  352.3 57.0 %all-reduce.3.cloned.1.call-start = ((), (), s32[]{:S(2)}) async-start(), calls=%async_computation.5 | async-start | bytes 1572864 | tf_op jit(solution)/shard_map/psum | solution.py:51
  364.6 50.1 %copy-start.2 = (f32[256,256]{1,0:T(8,128)}, f32[256,256]{1,0:T(8,128)S(1)}, u32[]{:S(2)}) copy-start(f32[256,256]{1,0:T(8,128)S(1)} %fusion.5) | copy-start | bytes 786436
  410.9 3.8 copy-start.3
  412.4 2.4 copy-start.4
Sparse Core Ops, SparseCore 0:
  12.3 83.3 all-gather.2
  136.8 148.2 reduce-scatter.1
  365.9 43.4 all-reduce.2
where the time goes:
time: 422 us; the launch traced here: 421 us
  waiting for transfers between devices  310 us (73%)
  local copies, waits for them, and re-layouts  47.2 us (11%)
  matrix products  36.8 us (9%)
  between operations  13.9 us (3%)
  starting transfers between devices  11 us (3%)
    reduce_scatter x1, waiting for transfers between devices, per_device(): reduced = lax.psum_scatter(terms, 'blk', scatter_dimension=1, tiled=True)  148 us
    all_gather x1, waiting for transfers between devices, per_device(): piece = lax.all_gather(stacked[None], 'sn', axis=0, tiled=True)  57.6 us
    all_to_all x1, waiting for transfers between devices, per_device(): lax.all_to_all(reduced, 'sn', split_axis=0, concat_axis=0, tiled=True)  52.6 us
    psum x1, waiting for transfers between devices, per_device(): diag_one = square_one + lax.psum(diag_term, 'blk')  42.3 us
    dot_general x1, matrix products, per_device(): jnp.einsum('rnkc,nkcd->nrd', chosen, panels, precision=lax.Precision.HIGH...  23.5 us
    all_gather x1, local copies, waits for them, and re-layouts, per_device(): piece = lax.all_gather(stacked[None], 'sn', axis=0, tiled=True)  17.5 us
    dot_general x11, matrix products, product(): jnp.dot(left, right, precision=lax.Precision.HIGHEST, preferred_element_t...  13.3 us
    unnamed x15, local copies, waits for them, and re-layouts  9.93 us
  transfers between devices with their start and end apart: 5, of which 5 were waited for; matrix products, arithmetic and copies ran while one was open for 7% of the time, Pallas kernels for 0%

commit v1 on v0

v1 whole, which is shorter than its diff:
```python
import functools

import jax
import jax.numpy as jnp
from jax import lax
from jax.experimental import pallas as pl
from jax.experimental.pallas import tpu as pltpu
from jax.sharding import PartitionSpec as P

MESH = pl.DeviceIdType.MESH
SIDE = 4
CORES = 2
POSITIONS = 4
PAIRS = tuple((i, k) for i in range(POSITIONS) for k in range(i, POSITIONS))
NP = len(PAIRS)
BLOCKS = 32
NEAR = BLOCKS // 2 + 1


def locate(a, b):
    d = jnp.bitwise_and(b - a + BLOCKS, BLOCKS - 1)
    swap = d >= NEAR
    return jnp.where(swap, b, a), jnp.where(swap, BLOCKS - d, d), swap


def place(row):
    return row // (SIDE * CORES), lax.rem(row // CORES, SIDE), lax.rem(row, CORES)


def exchange_kernel(
    pairs_ref, root, panel_one, panel_two, zed, panels,
    ag_a, ag_b, send_a, send_b, recv_a, recv_b,
    own_sem, pan_local, pan_send, pan_recv, ring_send, ring_recv,
    core_send, core_recv, sel_send, sel_recv, z_send, z_recv,
):
    width = panel_one.shape[0]
    quarter = width // SIDE
    half = quarter // 2
    sn = lax.axis_index("sn")
    z = lax.axis_index("blk")
    x, y, c = place(sn)

    def at(xx, yy, cc):
        return (xx * SIDE + yy) * CORES + cc

    def turn(v, o):
        return lax.rem(v + o, SIDE)

    x_dev = [(at(turn(x, o), y, c), z) for o in range(SIDE)]
    y_dev = [(at(x, turn(y, o), c), z) for o in range(SIDE)]
    z_dev = [(sn, turn(z, o)) for o in range(SIDE)]
    twin = (at(x, y, 1 - c), z)

    slot_a = x * CORES + c
    slot_b = y * CORES + c
    loads = []
    for h, (buf, slot) in enumerate(((ag_a, slot_a), (ag_b, slot_b))):
        for d in range(NEAR):
            col = lax.rem(sn + d, BLOCKS)
            cp = pltpu.make_async_copy(
                root.at[pl.ds(pl.multiple_of(z * quarter + h * half, half), half), pl.ds(pl.multiple_of(col * width, width), width)],
                buf.at[slot * NEAR + d],
                own_sem.at[h, d],
            )
            cp.start()
            loads.append(cp)
    pan = []
    for n, src in enumerate((panel_one, panel_two)):
        cp = pltpu.make_async_copy(src, panels.at[z, n], pan_local.at[n])
        cp.start()
        pan.append(cp)

    barrier = pltpu.get_barrier_semaphore()
    partners = x_dev[1:] + y_dev[1:] + z_dev[1:] + [twin]
    for dev in partners:
        pl.semaphore_signal(barrier, inc=1, device_id=dev, device_id_type=MESH)
    pl.semaphore_wait(barrier, len(partners))

    def remote(src, dst, ssem, rsem, dev):
        return pltpu.make_async_remote_copy(
            src_ref=src, dst_ref=dst, send_sem=ssem, recv_sem=rsem, device_id=dev, device_id_type=MESH
        )

    pan_out = []
    for o in range(1, SIDE):
        for n, src in enumerate((panel_one, panel_two)):
            cp = remote(src, panels.at[z, n], pan_send.at[o - 1, n], pan_recv.at[o - 1, n], z_dev[o])
            cp.start()
            pan_out.append(cp)

    lanes = []
    for h, (buf, pos, devs) in enumerate(((ag_a, x, x_dev), (ag_b, y, y_dev))):
        for cp in loads[h * NEAR:(h + 1) * NEAR]:
            cp.wait()

        def piece(o, lo=0, n=NEAR, buf=buf, pos=pos):
            return buf.at[pl.ds((turn(pos, o) * CORES + c) * NEAR + lo, n)]

        def theirs(o, lo=0, n=NEAR, buf=buf, pos=pos):
            return buf.at[pl.ds((turn(pos, o) * CORES + (1 - c)) * NEAR + lo, n)]

        up = remote(piece(0), piece(0), ring_send.at[h, 0], ring_recv.at[h, 0], devs[1])
        down = remote(piece(0), piece(0), ring_send.at[h, 1], ring_recv.at[h, 1], devs[3])
        side = remote(piece(0), piece(0), core_send.at[h, 0], core_recv.at[h, 0], twin)
        up.start()
        down.start()
        side.start()
        lanes.append((piece, theirs, up, down, side, devs))

    split = (NEAR + 1) // 2
    spans = ((0, split), (split, NEAR - split))
    started = []
    for h, (piece, theirs, up, down, side, devs) in enumerate(lanes):
        remote(piece(3), piece(3), ring_send.at[h, 0], ring_recv.at[h, 0], devs[1]).wait_recv()
        f_up = remote(piece(3, *spans[0]), piece(3, *spans[0]), ring_send.at[h, 2], ring_recv.at[h, 2], devs[1])
        f_up.start()
        s_up = remote(piece(3), piece(3), core_send.at[h, 1], core_recv.at[h, 1], twin)
        s_up.start()
        remote(piece(1), piece(1), ring_send.at[h, 1], ring_recv.at[h, 1], devs[3]).wait_recv()
        f_down = remote(piece(1, *spans[1]), piece(1, *spans[1]), ring_send.at[h, 3], ring_recv.at[h, 3], devs[3])
        f_down.start()
        s_down = remote(piece(1), piece(1), core_send.at[h, 2], core_recv.at[h, 2], twin)
        s_down.start()
        started.append([up, down, side, f_up, s_up, f_down, s_down])
    for h, (piece, theirs, up, down, side, devs) in enumerate(lanes):
        for part in range(2):
            remote(piece(2, *spans[part]), piece(2, *spans[part]), ring_send.at[h, 2 + part], ring_recv.at[h, 2 + part], devs[1]).wait_recv()
            s = remote(piece(2, *spans[part]), piece(2, *spans[part]), core_send.at[h, 3 + part], core_recv.at[h, 3 + part], twin)
            s.start()
            started[h].append(s)

    sel = []
    for h, (buf, send, recv, devs, pos, other) in enumerate(
        ((ag_a, send_a, recv_a, y_dev, y, x), (ag_b, send_b, recv_b, x_dev, x, y))
    ):
        piece, theirs = lanes[h][:2]
        for n, (o, lo, cnt) in enumerate(((0, 0, NEAR), (3, 0, NEAR), (1, 0, NEAR), (2, *spans[0]), (2, *spans[1]))):
            remote(theirs(o, lo, cnt), theirs(o, lo, cnt), core_send.at[h, n], core_recv.at[h, n], twin).wait_recv()
        for o in (2, 1, 3, 0):
            to = turn(pos, o)
            item = at(other, to, c) if h == 0 else at(to, other, c)

            def pick(p, carry, h=h, o=o, item=item, buf=buf, send=send, recv=recv, pos=pos):
                i = jnp.where(p < 4, 0, jnp.where(p < 7, 1, jnp.where(p < 9, 2, 3)))
                k = jnp.where(p < 4, p, jnp.where(p < 7, p - 3, jnp.where(p < 9, p - 5, 3)))
                row, dist, _ = locate(pairs_ref[item, i], pairs_ref[item, k])
                rx, ry, rc = place(row)
                slot = ((rx if h == 0 else ry) * CORES + rc) * NEAR + dist
                got = buf[slot]
                if o == 0:
                    recv[pos * NP + p] = got
                else:
                    send[(o - 1) * NP + p] = got
                return carry

            lax.fori_loop(0, NP, pick, 0)
            if o:
                cp = remote(
                    send.at[pl.ds((o - 1) * NP, NP)], recv.at[pl.ds(pos * NP, NP)],
                    sel_send.at[h, o - 1], sel_recv.at[h, o - 1], devs[o],
                )
                cp.start()
                sel.append(cp)
    for h, (send, recv, devs, pos) in enumerate(((send_a, recv_a, y_dev, y), (send_b, recv_b, x_dev, x))):
        for o in range(1, SIDE):
            frm = turn(pos, SIDE - o)
            remote(
                send.at[pl.ds((o - 1) * NP, NP)], recv.at[pl.ds(frm * NP, NP)],
                sel_send.at[h, o - 1], sel_recv.at[h, o - 1], devs[o],
            ).wait_recv()

    def keep(p, carry):
        i = jnp.where(p < 4, 0, jnp.where(p < 7, 1, jnp.where(p < 9, 2, 3)))
        k = jnp.where(p < 4, p, jnp.where(p < 7, p - 3, jnp.where(p < 9, p - 5, 3)))
        row, _, _ = locate(pairs_ref[sn, i], pairs_ref[sn, k])
        rx, ry, _ = place(row)
        zed[z * NP + p, 0:half] = recv_a[ry * NP + p]
        zed[z * NP + p, half:quarter] = recv_b[rx * NP + p]
        return carry

    lax.fori_loop(0, NP, keep, 0)

    def zpart(o, lo=0, n=NP):
        return zed.at[pl.ds(turn(z, o) * NP + lo, n)]

    zspans = ((0, NP // 2), (NP // 2, NP - NP // 2))
    zup = remote(zpart(0), zpart(0), z_send.at[0], z_recv.at[0], z_dev[1])
    zdown = remote(zpart(0), zpart(0), z_send.at[1], z_recv.at[1], z_dev[3])
    zup.start()
    zdown.start()
    remote(zpart(3), zpart(3), z_send.at[0], z_recv.at[0], z_dev[1]).wait_recv()
    fup = remote(zpart(3, *zspans[0]), zpart(3, *zspans[0]), z_send.at[2], z_recv.at[2], z_dev[1])
    fup.start()
    remote(zpart(1), zpart(1), z_send.at[1], z_recv.at[1], z_dev[3]).wait_recv()
    fdown = remote(zpart(1, *zspans[1]), zpart(1, *zspans[1]), z_send.at[3], z_recv.at[3], z_dev[3])
    fdown.start()
    for part in range(2):
        remote(zpart(2, *zspans[part]), zpart(2, *zspans[part]), z_send.at[2 + part], z_recv.at[2 + part], z_dev[1]).wait_recv()
    for o in range(1, SIDE):
        for n, src in enumerate((panel_one, panel_two)):
            remote(src, panels.at[turn(z, SIDE - o), n], pan_send.at[o - 1, n], pan_recv.at[o - 1, n], z_dev[o]).wait_recv()
    for cp in pan:
        cp.wait()
    for cp in pan_out + started[0] + started[1] + sel + [zup, zdown, fup, fdown]:
        cp.wait_send()


def exchange(structure, root, panel_one, panel_two):
    width = panel_one.shape[0]
    quarter, half = width // SIDE, width // SIDE // 2
    f32 = jnp.float32
    dma = pltpu.SemaphoreType.DMA
    anywhere = pl.BlockSpec(memory_space=pl.ANY)
    return pl.pallas_call(
        exchange_kernel,
        out_shape=(
            jax.ShapeDtypeStruct((SIDE * NP, quarter, width), f32),
            jax.ShapeDtypeStruct((SIDE, 2, width, width), f32),
        ),
        in_specs=[pl.BlockSpec(memory_space=pltpu.SMEM), anywhere, anywhere, anywhere],
        out_specs=(pl.BlockSpec(memory_space=pltpu.VMEM), anywhere),
        scratch_shapes=[
            pltpu.VMEM((SIDE * CORES * NEAR, half, width), f32),
            pltpu.VMEM((SIDE * CORES * NEAR, half, width), f32),
            pltpu.VMEM(((SIDE - 1) * NP, half, width), f32),
            pltpu.VMEM(((SIDE - 1) * NP, half, width), f32),
            pltpu.VMEM((SIDE * NP, half, width), f32),
            pltpu.VMEM((SIDE * NP, half, width), f32),
            dma((2, NEAR)),
            dma((2,)),
            dma((SIDE - 1, 2)),
            dma((SIDE - 1, 2)),
            dma((2, 4)),
            dma((2, 4)),
            dma((2, 5)),
            dma((2, 5)),
            dma((2, SIDE - 1)),
            dma((2, SIDE - 1)),
            dma((4,)),
            dma((4,)),
        ],
        compiler_params=pltpu.CompilerParams(
            collective_id=0, has_side_effects=True, vmem_limit_bytes=40 * 2**20
        ),
        name="exchange",
    )(structure, root, panel_one, panel_two)


def parts(v):
    high = v.astype(jnp.bfloat16)
    return high, (v - high.astype(jnp.float32)).astype(jnp.bfloat16)


def mul(a, b, ca=1, cb=0):
    dims = (((ca,), (cb,)), ((), ()))
    dot = functools.partial(lax.dot_general, dimension_numbers=dims, preferred_element_type=jnp.float32)
    return dot(a[0], b[0]) + (dot(a[0], b[1]) + dot(a[1], b[0]))


def finish_kernel(
    structure, zed, panels, inverse_one, parent, inverse_two,
    diag_one, off_one, diag_two, par_two, root_two,
    u_high, u_low, w,
):
    width = inverse_one.shape[0]
    sn = lax.axis_index("sn")
    z = lax.axis_index("blk")
    inv_one = parts(inverse_one[...])
    inv_two = parts(inverse_two[...])
    for k in range(POSITIONS):
        for n, inv in enumerate((inv_one, inv_two)):
            high, low = parts(mul(parts(panels[k, n]), inv))
            u_high[k, :, n * width:(n + 1) * width] = high
            u_low[k, :, n * width:(n + 1) * width] = low
    u_par = parts(mul(parts(parent[...]), inv_two))
    w[...] = jnp.zeros_like(w)
    for p, (i, k) in enumerate(PAIRS):
        block = jnp.concatenate([zed[q * NP + p] for q in range(SIDE)], axis=0)
        block = parts(block)
        if i == k:
            w[i] += mul(block, (u_high[i], u_low[i]))
            continue
        _, _, swap = locate(structure[sn, i], structure[sn, k])
        major = jnp.where(swap, k, i)
        minor = jnp.where(swap, i, k)
        w[major] += mul(block, (u_high[minor], u_low[minor]))
        w[minor] += mul(block, (u_high[major], u_low[major]), 0, 0)
    uu_one = uu_mixed = uu_two = 0.0
    for k in range(POSITIONS):
        one = (u_high[k, :, :width], u_low[k, :, :width])
        two = (u_high[k, :, width:], u_low[k, :, width:])
        w_one = parts(w[k, :, :width])
        w_two = parts(w[k, :, width:])
        uu_one = uu_one + mul(one, w_one, 0, 0)
        uu_mixed = uu_mixed + mul(two, w_one, 0, 0)
        uu_two = uu_two + mul(two, w_two, 0, 0)
    d_one = mul(inv_one, inv_one, 0, 0) + uu_one
    diag_one[...] = d_one
    own_one = w[z, :, :width]
    off_one[...] = -own_one
    root_two[...] = mul(parts(own_one), u_par) - w[z, :, width:]
    p_two = uu_mixed.T - mul(parts(d_one), u_par)
    par_two[...] = p_two
    child = mul(parts(uu_mixed), u_par) - uu_two
    diag_two[...] = mul(inv_two, inv_two, 0, 0) - mul(u_par, parts(p_two), 0, 0) - child


def finish(structure, zed, panels, inverse_one, parent, inverse_two):
    width = inverse_one.shape[0]
    vmem = pl.BlockSpec(memory_space=pltpu.VMEM)
    square = jax.ShapeDtypeStruct((width, width), jnp.float32)
    return pl.pallas_call(
        finish_kernel,
        out_shape=(square,) * 5,
        in_specs=[pl.BlockSpec(memory_space=pltpu.SMEM)] + [vmem] * 5,
        out_specs=(vmem,) * 5,
        scratch_shapes=[
            pltpu.VMEM((POSITIONS, width, 2 * width), jnp.bfloat16),
            pltpu.VMEM((POSITIONS, width, 2 * width), jnp.bfloat16),
            pltpu.VMEM((POSITIONS, width, 2 * width), jnp.float32),
        ],
        compiler_params=pltpu.CompilerParams(vmem_limit_bytes=40 * 2**20),
        name="finish",
    )(structure, zed, panels, inverse_one, parent, inverse_two)


def per_device(root_inverse, structure, panel_one, inverse_one, parent_two, panel_two, inverse_two):
    zed, panels = exchange(structure, root_inverse, panel_one[0], panel_two[0])
    outs = finish(structure, zed, panels, inverse_one[0], parent_two[0], inverse_two[0])
    return tuple(out[None] for out in outs)


def solution(mesh):
    return jax.shard_map(
        per_device,
        mesh=mesh,
        in_specs=(
            P("sn", None),
            P(),
            P("sn", "blk", None),
            P("sn", None, None),
            P("sn", None, None),
            P("sn", "blk", None),
            P("sn", None, None),
        ),
        out_specs=(
            P("sn", None, None),
            P("sn", "blk", None),
            P("sn", None, None),
            P("sn", None, None),
            P("sn", "blk", None),
        ),
        check_vma=False,
    )
```

time: 422 us -> 91.5 us (0.22)
  waiting for transfers between devices: 310 us -> 0 us
  Pallas kernels: 0 us -> 84.5 us
  local copies, waits for them, and re-layouts: 47.2 us -> 6.05 us
  matrix products: 36.8 us -> 0 us
  between operations: 13.9 us -> 0.67 us
  starting transfers between devices: 11 us -> 0 us
    reduce_scatter x1 -> x0, waiting for transfers between devices: 148 us -> none  [per_device(): reduced = lax.psum_scatter(terms, 'blk', scatter_dimension=1, tiled=True)]
    pallas_call x0 -> x2, Pallas kernels: none -> 84.5 us  [the longest x1 74 us: exchange(): pl.pallas_call(exchange_kernel, out_shape=(jax.ShapeDtypeStruct((SIDE * N...]
    all_to_all x2 -> x0, waiting for transfers between devices: 61.5 us -> none  [the longest x1 52.6 us: per_device(): lax.all_to_all(reduced, 'sn', split_axis=0, concat_axis=0, tiled=True)]
    all_gather x1 -> x0, waiting for transfers between devices: 57.6 us -> none  [per_device(): piece = lax.all_gather(stacked[None], 'sn', axis=0, tiled=True)]
    psum x1 -> x0, waiting for transfers between devices: 42.3 us -> none  [per_device(): diag_one = square_one + lax.psum(diag_term, 'blk')]
    dot_general x12 -> x0, matrix products: 36.8 us -> none  [the longest x1 23.5 us: per_device(): jnp.einsum('rnkc,nkcd->nrd', chosen, panels, precision=lax.Precision.HIGH...]
    all_gather x1 -> x0, local copies, waits for them, and re-layouts: 17.5 us -> none  [per_device(): piece = lax.all_gather(stacked[None], 'sn', axis=0, tiled=True)]
    all_to_all x2 -> x0, starting transfers between devices: 10.7 us -> none  [the longest x1 7.22 us: per_device(): lax.all_to_all(reduced, 'sn', split_axis=0, concat_axis=0, tiled=True)]
  transfers between devices with their start and end apart: 5 -> 0, of which waited for: 5 -> 0; matrix products, arithmetic and copies ran while one was open for 7% -> 0% of each run, Pallas kernels for 0% -> 0%
where the time goes in v1:
time: 91.5 us; the launch traced here: 91.3 us
  Pallas kernels  84.5 us (92%)
  local copies, waits for them, and re-layouts  6.05 us (7%)
    pallas_call x1, Pallas kernels, exchange(): pl.pallas_call(exchange_kernel, out_shape=(jax.ShapeDtypeStruct((SIDE * N...  74 us
    pallas_call x1, Pallas kernels, finish(): pl.pallas_call(finish_kernel, out_shape=(square,) * 5, in_specs=[pl.Block...  10.6 us
    unnamed x13, local copies, waits for them, and re-layouts  6.05 us

profile of v1, /device:TPU:0, one launch (start us, length us, event | category | flops | bytes accessed | tf_op | source)
XLA Modules:
  0.0 91.3 jit_solution(4642994391250427635)
XLA Ops:
  0.6 0.8 copy.13.pairs_ref.structure
  1.4 0.0 copy-start
  1.4 3.4 %copy-done = f32[256,8192]{1,0:T(8,128)S(1)} copy-done((f32[256,8192]{1,0:T(8,128)S(1)}, f32[256,8192]{1,0:T(8,128)}, u32[]{:S(2)}) %copy-start) | copy-done | bytes 8388632
  4.8 0.0 copy-start.1
  4.8 0.9 %copy-done.1 = f32[1,256,256]{2,1,0:T(8,128)S(1)} copy-done((f32[1,256,256]{2,1,0:T(8,128)S(1)}, f32[1,256,256]{2,1,0:T(8,128)}, u32[]{:S(2)}) %copy-start.1) | copy-done | bytes 262168
  5.7 0.0 copy-start.2
  5.7 0.9 %copy-done.2 = f32[1,256,256]{2,1,0:T(8,128)S(1)} copy-done((f32[1,256,256]{2,1,0:T(8,128)S(1)}, f32[1,256,256]{2,1,0:T(8,128)}, u32[]{:S(2)}) %copy-start.2) | copy-done | bytes 262168
  6.7 0.0 copy-start.3
  6.7 0.0 copy-start.4
  6.7 0.0 copy-start.5
  6.7 74.0 %exchange.1 = (f32[40,64,256]{2,1,0:T(8,128)S(1)}, f32[4,2,256,256]{3,2,1,0:T(8,128)S(1)}) custom-call(s32[32,4]{1,0:T(8,128)S(1)} %copy.13.pairs_ref.structure, f32[256,8192]{1,0:T(8,128)S(1)} %copy-done, f32[256,256]{1,0:T(8,128)S(1)} %bitcast.10, f32[256,256]{1,0:T(8,128)S(1)} %bitcast.11), custom_call_target="tpu_custom_call" | custom-call | tf_op jit(solution)/shard_map/exchange/pallas_call | solution.py:214
  80.7 0.0 copy-done.3
  80.7 0.0 copy-done.4
  80.7 0.0 copy-done.5
  80.7 10.6 %finish.1 = (f32[256,256]{1,0:T(8,128)}, f32[256,256]{1,0:T(8,128)}, f32[256,256]{1,0:T(8,128)}, f32[256,256]{1,0:T(8,128)}, f32[256,256]{1,0:T(8,128)}) custom-call(s32[32,4]{1,0:T(8,128)S(1)} %copy.13.pairs_ref.structure, f32[40,64,256]{2,1,0:T(8,128)S(1)} %get-tuple-element.12.zed, f32[4,2,256,256]{3,2,1,0:T(8,128)S(1)} %get-tuple-element.13.panels, ...), custom_call_target="tpu_custom_call" | custom-call | tf_op jit(solution)/shard_map/finish/pallas_call | solution.py:312
Async XLA Ops:
  1.4 3.4 %copy-start = (f32[256,8192]{1,0:T(8,128)S(1)}, f32[256,8192]{1,0:T(8,128)}, u32[]{:S(2)}) copy-start(f32[256,8192]{1,0:T(8,128)} %root.1) | copy-start | bytes 25165828
  4.8 0.9 %copy-start.1 = (f32[1,256,256]{2,1,0:T(8,128)S(1)}, f32[1,256,256]{2,1,0:T(8,128)}, u32[]{:S(2)}) copy-start(f32[1,256,256]{2,1,0:T(8,128)} %param.9) | copy-start | bytes 786436
  5.7 0.9 %copy-start.2 = (f32[1,256,256]{2,1,0:T(8,128)S(1)}, f32[1,256,256]{2,1,0:T(8,128)}, u32[]{:S(2)}) copy-start(f32[1,256,256]{2,1,0:T(8,128)} %param.12) | copy-start | bytes 786436
  6.7 74.0 %copy-start.3 = (f32[1,256,256]{2,1,0:T(8,128)S(1)}, f32[1,256,256]{2,1,0:T(8,128)}, u32[]{:S(2)}) copy-start(f32[1,256,256]{2,1,0:T(8,128)} %param.10) | copy-start | bytes 786436
  6.7 74.0 %copy-start.4 = (f32[1,256,256]{2,1,0:T(8,128)S(1)}, f32[1,256,256]{2,1,0:T(8,128)}, u32[]{:S(2)}) copy-start(f32[1,256,256]{2,1,0:T(8,128)} %param.11) | copy-start | bytes 786436
  6.7 74.0 %copy-start.5 = (f32[1,256,256]{2,1,0:T(8,128)S(1)}, f32[1,256,256]{2,1,0:T(8,128)}, u32[]{:S(2)}) copy-start(f32[1,256,256]{2,1,0:T(8,128)} %param.13) | copy-start | bytes 786436

commit v2 on v0

v2 whole, which is shorter than its diff:
```python
import functools

import jax
import jax.numpy as jnp
from jax import lax
from jax.experimental import pallas as pl
from jax.experimental.pallas import tpu as pltpu
from jax.sharding import PartitionSpec as P

MESH = pl.DeviceIdType.MESH
SIDE = 4
CORES = 2
POSITIONS = 4
PAIRS = tuple((i, k) for i in range(POSITIONS) for k in range(i, POSITIONS))
NP = len(PAIRS)
BLOCKS = 32
NEAR = BLOCKS // 2 + 1


def locate(a, b):
    d = jnp.bitwise_and(b - a + BLOCKS, BLOCKS - 1)
    swap = d >= NEAR
    return jnp.where(swap, b, a), jnp.where(swap, BLOCKS - d, d), swap


def parts(v):
    high = v.astype(jnp.bfloat16)
    return high, (v - high.astype(jnp.float32)).astype(jnp.bfloat16)


def mul(a, b, ca=1, cb=0):
    dims = (((ca,), (cb,)), ((), ()))
    dot = functools.partial(lax.dot_general, dimension_numbers=dims, preferred_element_type=jnp.float32)
    return dot(a[0], b[0]) + (dot(a[0], b[1]) + dot(a[1], b[0]))


def place(row):
    return row // (SIDE * CORES), lax.rem(row // CORES, SIDE), lax.rem(row, CORES)


def exchange_kernel(
    structure, root, panel_one, panel_two, inverse_one, parent, inverse_two,
    own_w, diag_one, mixed, rest_two, par,
    zed, loaded, u_all, u_high, u_low, w, table, rows, ag_a, ag_b, main_out, main_in, own_in, relay_out, relay_in,
    root_sem, load_sem, pan_send, pan_recv, pan_fsend, pan_frecv,
    ring_send, ring_recv, fwd_send, fwd_recv, core_send, core_recv,
    relay_send, relay_recv, main_send, main_recv, z_send, z_recv, zf_send, zf_recv,
):
    width = panel_one.shape[0]
    quarter = width // SIDE
    half = quarter // 2
    sn = lax.axis_index("sn")
    z = lax.axis_index("blk")
    x, y, c = place(sn)

    def at(xx, yy, cc):
        return (xx * SIDE + yy) * CORES + cc

    def turn(v, o):
        return lax.rem(v + o, SIDE)

    x_dev = [(at(turn(x, o), y, c), z) for o in range(SIDE)]
    y_dev = [(at(x, turn(y, o), c), z) for o in range(SIDE)]
    z_dev = [(sn, turn(z, o)) for o in range(SIDE)]
    twin = (at(x, y, 1 - c), z)
    UP, DOWN = 0, 1
    BELOW, ABOVE = 3, 1
    step = (1, 3)

    own_rows = pltpu.make_async_copy(
        root.at[pl.ds(pl.multiple_of(z * quarter, quarter), quarter), :], rows, root_sem
    )
    own_rows.start()
    loads = [
        pltpu.make_async_copy(src, loaded.at[n], load_sem.at[n])
        for n, src in enumerate((panel_one, inverse_one, panel_two, inverse_two, parent))
    ]
    for cp in loads:
        cp.start()

    barrier = pltpu.get_barrier_semaphore()
    partners = [x_dev[1], x_dev[3], y_dev[1], y_dev[3], z_dev[1], z_dev[3], twin]
    for dev in partners:
        pl.semaphore_signal(barrier, inc=1, device_id=dev, device_id_type=MESH)
    pl.semaphore_wait(barrier, len(partners))

    sent = []

    def remote(src, dst, ssem, rsem, dev):
        return pltpu.make_async_remote_copy(
            src_ref=src, dst_ref=dst, send_sem=ssem, recv_sem=rsem, device_id=dev, device_id_type=MESH
        )

    def push(*what):
        cp = remote(*what)
        cp.start()
        sent.append(cp)

    own_rows.wait()
    split = (NEAR + 1) // 2
    spans = ((0, split), (split, NEAR - split))
    axes = ((ag_a, x, x_dev), (ag_b, y, y_dev))

    def piece(h, o, s, core):
        buf, pos, _ = axes[h]
        return buf.at[pl.ds((turn(pos, o) * CORES + core) * NEAR + spans[s][0], spans[s][1])]

    def share(h, o, s):
        push(piece(h, o, s, c), piece(h, o, s, c), core_send.at[h, o, s], core_recv.at[h, o, s], twin)

    for h in range(2):
        buf, pos, devs = axes[h]
        base = (pos * CORES + c) * NEAR

        def reblock(d, carry, h=h, buf=buf, base=base):
            col = pl.multiple_of(lax.rem(sn + d, BLOCKS) * width, width)
            buf[base + d] = rows[h * half:(h + 1) * half, pl.ds(col, width)]
            return carry

        lax.fori_loop(0, NEAR, reblock, 0)
        for order in range(2):
            for e in range(2):
                s = (order, 1 - order)[e]
                push(piece(h, 0, s, c), piece(h, 0, s, c), ring_send.at[h, e, s], ring_recv.at[h, e, s], devs[step[e]])
        for s in range(2):
            share(h, 0, s)

    for cp in loads:
        cp.wait()
    inv_one, inv_two = parts(loaded[1]), parts(loaded[3])
    u_all[z, 0] = mul(parts(loaded[0]), inv_one)
    u_all[z, 1] = mul(parts(loaded[2]), inv_two)

    def u_part(o, n):
        return u_all.at[turn(z, o), n]

    for order in range(2):
        for e in range(2):
            n = (order, 1 - order)[e]
            push(u_part(0, n), u_part(0, n), pan_send.at[e, n], pan_recv.at[e, n], z_dev[step[e]])

    def fill(n, carry):
        o = lax.rem(n, SIDE)
        along_x = n // SIDE
        item = at(turn(x, o * along_x), turn(y, o * (1 - along_x)), c)
        for p, (i, k) in enumerate(PAIRS):
            row, dist, swap = locate(structure[item, i], structure[item, k])
            rx, ry, rc = place(row)
            table[n, p] = (jnp.where(along_x == 0, rx, ry) * CORES + rc) * NEAR + dist
            table[n, NP + p] = jnp.where(along_x == 0, ry, rx)
            table[n, 2 * NP + p] = swap.astype(jnp.int32)
        return carry

    lax.fori_loop(0, 2 * SIDE, fill, 0)

    def ring_wait(h, e, s):
        o = (BELOW, ABOVE)[e]
        remote(piece(h, o, s, c), piece(h, o, s, c), ring_send.at[h, e, s], ring_recv.at[h, e, s], axes[h][2][step[e]]).wait_recv()
        return o

    for h in range(2):
        for e in range(2):
            o = ring_wait(h, e, e)
            push(piece(h, o, e, c), piece(h, o, e, c), fwd_send.at[h, e], fwd_recv.at[h, e], axes[h][2][step[e]])
            share(h, o, e)
    def split_u(o):
        for n in range(2):
            at_k = turn(z, o)
            u_high[at_k, :, n * width:(n + 1) * width], u_low[at_k, :, n * width:(n + 1) * width] = parts(u_all[at_k, n])

    u_par = mul(parts(loaded[4]), inv_two)
    par[...] = u_par
    for e in range(2):
        o = (BELOW, ABOVE)[e]
        remote(u_part(o, e), u_part(o, e), pan_send.at[e, e], pan_recv.at[e, e], z_dev[step[e]]).wait_recv()
        push(u_part(o, e), u_part(o, e), pan_fsend.at[e], pan_frecv.at[e], z_dev[step[e]])
    split_u(0)
    for h in range(2):
        for e in range(2):
            share(h, ring_wait(h, e, 1 - e), 1 - e)
    diag_one[...] = mul(inv_one, inv_one, 0, 0)
    rest_two[...] = mul(inv_two, inv_two, 0, 0)
    for h in range(2):
        for e in range(2):
            remote(piece(h, 2, e, c), piece(h, 2, e, c), fwd_send.at[h, e], fwd_recv.at[h, e], axes[h][2][step[e]]).wait_recv()
            share(h, 2, e)

    for h in range(2):
        for o in (0, BELOW, ABOVE, 2):
            for s in range(2):
                remote(piece(h, o, s, 1 - c), piece(h, o, s, 1 - c), core_send.at[h, o, s], core_recv.at[h, o, s], twin).wait_recv()
    routes = ((ag_a, y, y_dev), (ag_b, x, x_dev))

    def pick(h, o, p):
        return routes[h][0][table[h * SIDE + o, p]]

    def owner(h, o, p):
        return table[h * SIDE + o, NP + p]

    half_pairs = NP // 2
    for h in range(2):
        devs = routes[h][2]
        for g in range(half_pairs):
            for e in range(2):
                relay_out[h, e, g] = pick(h, 2, 2 * g + e)
                push(
                    relay_out.at[h, e, g], relay_in.at[h, e, g],
                    relay_send.at[h, e, g], relay_recv.at[h, e, g], devs[step[e]],
                )
    for h in range(2):
        for p in range(NP):
            own_in[h, p] = pick(h, 0, p)
    for g in range(half_pairs):
        for h in range(2):
            pos, devs = routes[h][1], routes[h][2]
            for e in range(2):
                o = step[e]
                remote(
                    relay_out.at[h, e, g], relay_in.at[h, e, g],
                    relay_send.at[h, e, g], relay_recv.at[h, e, g], devs[o],
                ).wait_recv()
                for q in range(2):
                    p = 2 * g + q
                    value = pick(h, o, p)
                    if q == e:
                        value = jnp.where(owner(h, o, p) == turn(pos, SIDE - o), relay_in[h, e, g], value)
                    main_out[h, e, p] = value
                push(
                    main_out.at[h, e, pl.ds(2 * g, 2)], main_in.at[h, e, pl.ds(2 * g, 2)],
                    main_send.at[h, e, g], main_recv.at[h, e, g], devs[o],
                )

    def zpart(o, lo, n):
        return zed.at[pl.ds(turn(z, o) * NP + lo, n)]

    def gather(g):
        for h in range(2):
            pos, devs = routes[h][1], routes[h][2]
            for e in range(2):
                remote(
                    main_out.at[h, e, pl.ds(2 * g, 2)], main_in.at[h, e, pl.ds(2 * g, 2)],
                    main_send.at[h, e, g], main_recv.at[h, e, g], devs[step[e]],
                ).wait_recv()
            for q in range(2):
                p = 2 * g + q
                who = owner(h, 0, p)
                below, above = main_in[h, UP, p], main_in[h, DOWN, p]
                far = below if q == UP else above
                value = jnp.where(who == pos, own_in[h, p], far)
                value = jnp.where(who == turn(pos, BELOW), below, value)
                value = jnp.where(who == turn(pos, ABOVE), above, value)
                zed[z * NP + p, h * half:(h + 1) * half] = value
        for e in range(2):
            push(zpart(0, 2 * g, 2), zpart(0, 2 * g, 2), z_send.at[e, g], z_recv.at[e, g], z_dev[step[e]])

    def hand_on(g):
        for e in range(2):
            o = (BELOW, ABOVE)[e]
            remote(zpart(o, 2 * g, 2), zpart(o, 2 * g, 2), z_send.at[e, g], z_recv.at[e, g], z_dev[step[e]]).wait_recv()
            push(zpart(o, 2 * g + e, 1), zpart(o, 2 * g + e, 1), zf_send.at[e, g], zf_recv.at[e, g], z_dev[step[e]])

    def arrive(g):
        for e in range(2):
            remote(zpart(2, 2 * g + e, 1), zpart(2, 2 * g + e, 1), zf_send.at[e, g], zf_recv.at[e, g], z_dev[step[e]]).wait_recv()

    def products(p):
        i, k = PAIRS[p]
        block = jnp.concatenate([zed[q * NP + p] for q in range(SIDE)], axis=0)
        flipped = block.T
        swap = table[0, 2 * NP + p] == 1
        direct = parts(jnp.where(swap, flipped, block))
        value = mul(direct, (u_high[k], u_low[k]))
        w[i] = value if i == 0 and k == 0 else w[i] + value
        if i != k:
            value = mul(parts(jnp.where(swap, block, flipped)), (u_high[i], u_low[i]))
            w[k] = value if i == 0 else w[k] + value
        if k == POSITIONS - 1:
            one = (u_high[i, :, :width], u_low[i, :, :width])
            two = (u_high[i, :, width:], u_low[i, :, width:])
            w_one, w_two = parts(w[i, :, :width]), parts(w[i, :, width:])
            diag_one[...] += mul(one, w_one, 0, 0)
            cross = mul(two, w_one, 0, 0)
            mixed[...] = cross if i == 0 else mixed[...] + cross
            rest_two[...] += mul(two, w_two, 0, 0)

    for e in range(2):
        n, o = 1 - e, (BELOW, ABOVE)[e]
        remote(u_part(o, n), u_part(o, n), pan_send.at[e, n], pan_recv.at[e, n], z_dev[step[e]]).wait_recv()
        remote(u_part(2, e), u_part(2, e), pan_fsend.at[e], pan_frecv.at[e], z_dev[step[e]]).wait_recv()
    for o in range(1, SIDE):
        split_u(o)
    for t in range(half_pairs + 2):
        if t < half_pairs:
            gather(t)
        if 1 <= t <= half_pairs:
            hand_on(t - 1)
        if t >= 2:
            arrive(t - 2)
            for q in range(2):
                products(2 * (t - 2) + q)
    own_w[...] = w[z]
    for cp in sent:
        cp.wait_send()


def exchange(structure, root, panel_one, panel_two, inverse_one, parent, inverse_two):
    width = panel_one.shape[0]
    quarter, half = width // SIDE, width // SIDE // 2
    f32 = jnp.float32
    dma = pltpu.SemaphoreType.DMA
    hbm = pl.BlockSpec(memory_space=pltpu.HBM)
    vmem = pl.BlockSpec(memory_space=pltpu.VMEM)
    groups = NP // 2
    square = jax.ShapeDtypeStruct((width, width), f32)
    return pl.pallas_call(
        exchange_kernel,
        out_shape=(jax.ShapeDtypeStruct((width, 2 * width), f32),) + (square,) * 4,
        in_specs=[pl.BlockSpec(memory_space=pltpu.SMEM)] + [hbm] * 6,
        out_specs=(vmem,) * 5,
        scratch_shapes=[
            pltpu.VMEM((SIDE * NP, quarter, width), f32),
            pltpu.VMEM((5, width, width), f32),
            pltpu.VMEM((POSITIONS, 2, width, width), f32),
            pltpu.VMEM((POSITIONS, width, 2 * width), jnp.bfloat16),
            pltpu.VMEM((POSITIONS, width, 2 * width), jnp.bfloat16),
            pltpu.VMEM((POSITIONS, width, 2 * width), f32),
            pltpu.SMEM((2 * SIDE, 3 * NP), jnp.int32),
            pltpu.VMEM((quarter, root.shape[1]), f32),
            pltpu.VMEM((SIDE * CORES * NEAR, half, width), f32),
            pltpu.VMEM((SIDE * CORES * NEAR, half, width), f32),
            pltpu.VMEM((2, 2, NP, half, width), f32),
            pltpu.VMEM((2, 2, NP, half, width), f32),
            pltpu.VMEM((2, NP, half, width), f32),
            pltpu.VMEM((2, 2, groups, half, width), f32),
            pltpu.VMEM((2, 2, groups, half, width), f32),
            dma,
            dma((5,)),
            dma((2, 2)), dma((2, 2)), dma((2,)), dma((2,)),
            dma((2, 2, 2)), dma((2, 2, 2)), dma((2, 2)), dma((2, 2)),
            dma((2, SIDE, 2)), dma((2, SIDE, 2)),
            dma((2, 2, groups)), dma((2, 2, groups)),
            dma((2, 2, groups)), dma((2, 2, groups)),
            dma((2, groups)), dma((2, groups)), dma((2, groups)), dma((2, groups)),
        ],
        compiler_params=pltpu.CompilerParams(
            collective_id=0, has_side_effects=True, vmem_limit_bytes=57 * 2**20
        ),
        name="exchange",
    )(structure, root, panel_one, panel_two, inverse_one, parent, inverse_two)


def finish_kernel(w, total_one, mixed, rest_two, par, diag_one, off_one, diag_two, par_two, root_two):
    width = par.shape[0]
    u_par = parts(par[...])
    w_one = w[:, :width]
    diag_one[...] = total_one[...]
    off_one[...] = -w_one
    root_two[...] = mul(parts(w_one), u_par) - w[:, width:]
    cross = mixed[...]
    p_two = cross.T - mul(parts(total_one[...]), u_par)
    par_two[...] = p_two
    diag_two[...] = rest_two[...] - mul(parts(cross), u_par) - mul(u_par, parts(p_two), 0, 0)


def finish(*args):
    vmem = pl.BlockSpec(memory_space=pltpu.VMEM)
    return pl.pallas_call(
        finish_kernel,
        out_shape=(jax.ShapeDtypeStruct(args[-1].shape, jnp.float32),) * 5,
        in_specs=[vmem] * 5,
        out_specs=(vmem,) * 5,
        compiler_params=pltpu.CompilerParams(vmem_limit_bytes=16 * 2**20),
        name="finish",
    )(*args)


def per_device(root_inverse, structure, panel_one, inverse_one, parent_two, panel_two, inverse_two):
    sums = exchange(
        structure, root_inverse, panel_one[0], panel_two[0], inverse_one[0], parent_two[0], inverse_two[0]
    )
    return tuple(out[None] for out in finish(*sums))


def solution(mesh):
    return jax.shard_map(
        per_device,
        mesh=mesh,
        in_specs=(
            P("sn", None),
            P(),
            P("sn", "blk", None),
            P("sn", None, None),
            P("sn", None, None),
            P("sn", "blk", None),
            P("sn", None, None),
        ),
        out_specs=(
            P("sn", None, None),
            P("sn", "blk", None),
            P("sn", None, None),
            P("sn", None, None),
            P("sn", "blk", None),
        ),
        check_vma=False,
    )
```

time: 422 us -> 78 us (0.18)
  waiting for transfers between devices: 310 us -> 0 us
  Pallas kernels: 0 us -> 70.5 us
  local copies, waits for them, and re-layouts: 47.2 us -> 6.2 us
  matrix products: 36.8 us -> 0 us
  between operations: 13.9 us -> 0.65 us
  starting transfers between devices: 11 us -> 0 us
    reduce_scatter x1 -> x0, waiting for transfers between devices: 148 us -> none  [per_device(): reduced = lax.psum_scatter(terms, 'blk', scatter_dimension=1, tiled=True)]
    pallas_call x0 -> x2, Pallas kernels: none -> 70.5 us  [the longest x1 69.1 us: exchange(): pl.pallas_call(exchange_kernel, out_shape=(jax.ShapeDtypeStruct((width, 2...]
    all_to_all x2 -> x0, waiting for transfers between devices: 61.5 us -> none  [the longest x1 52.6 us: per_device(): lax.all_to_all(reduced, 'sn', split_axis=0, concat_axis=0, tiled=True)]
    all_gather x1 -> x0, waiting for transfers between devices: 57.6 us -> none  [per_device(): piece = lax.all_gather(stacked[None], 'sn', axis=0, tiled=True)]
    psum x1 -> x0, waiting for transfers between devices: 42.3 us -> none  [per_device(): diag_one = square_one + lax.psum(diag_term, 'blk')]
    dot_general x12 -> x0, matrix products: 36.8 us -> none  [the longest x1 23.5 us: per_device(): jnp.einsum('rnkc,nkcd->nrd', chosen, panels, precision=lax.Precision.HIGH...]
    all_gather x1 -> x0, local copies, waits for them, and re-layouts: 17.5 us -> none  [per_device(): piece = lax.all_gather(stacked[None], 'sn', axis=0, tiled=True)]
    all_to_all x2 -> x0, starting transfers between devices: 10.7 us -> none  [the longest x1 7.22 us: per_device(): lax.all_to_all(reduced, 'sn', split_axis=0, concat_axis=0, tiled=True)]
  transfers between devices with their start and end apart: 5 -> 0, of which waited for: 5 -> 0; matrix products, arithmetic and copies ran while one was open for 7% -> 0% of each run, Pallas kernels for 0% -> 0%
where the time goes in v2:
time: 78 us; the launch traced here: 77.4 us
  Pallas kernels  70.5 us (90%)
  local copies, waits for them, and re-layouts  6.2 us (8%)
    pallas_call x1, Pallas kernels, exchange(): pl.pallas_call(exchange_kernel, out_shape=(jax.ShapeDtypeStruct((width, 2...  69.1 us
    unnamed x11, local copies, waits for them, and re-layouts  6.2 us

profile of v2, /device:TPU:0, one launch (start us, length us, event | category | flops | bytes accessed | tf_op | source)
XLA Modules:
  0.0 77.4 jit_solution(270204796505363486)
XLA Ops:
  0.6 1.4 %copy.12.structure = s32[32,4]{1,0:T(8,128)} copy(s32[32,4]{0,1:T(4,128)} %param.8) | data formatting | bytes 1024 | tf_op args[1]
  2.0 69.1 %exchange.1 = (f32[256,512]{1,0:T(8,128)}, f32[256,256]{1,0:T(8,128)}, f32[256,256]{1,0:T(8,128)}, f32[256,256]{1,0:T(8,128)}, f32[256,256]{1,0:T(8,128)}) custom-call(s32[32,4]{1,0:T(8,128)} %copy.12.structure, f32[256,8192]{1,0:T(8,128)} %root.1, f32[256,256]{1,0:T(8,128)} %bitcast.10, f32[256,256]{1,0:T(8,128)} %bitcast.11, f32[256,256]{1,0:T(8,128)} %bitcast.12, ...), custom_call_target="tpu_custom_call" | custom-call | tf_op jit(solution)/shard_map/exchange/pallas_call | solution.py:315
  71.1 0.0 copy-start
  71.1 1.0 %copy-done = f32[256,512]{1,0:T(8,128)S(1)} copy-done((f32[256,512]{1,0:T(8,128)S(1)}, f32[256,512]{1,0:T(8,128)}, u32[]{:S(2)}) %copy-start) | copy-done | bytes 524312
  72.1 0.0 copy-start.1
  72.1 0.9 %copy-done.1 = f32[256,256]{1,0:T(8,128)S(1)} copy-done((f32[256,256]{1,0:T(8,128)S(1)}, f32[256,256]{1,0:T(8,128)}, u32[]{:S(2)}) %copy-start.1) | copy-done | bytes 262168
  73.1 0.0 copy-start.2
  73.1 0.9 %copy-done.2 = f32[256,256]{1,0:T(8,128)S(1)} copy-done((f32[256,256]{1,0:T(8,128)S(1)}, f32[256,256]{1,0:T(8,128)}, u32[]{:S(2)}) %copy-start.2) | copy-done | bytes 262168
  74.0 0.0 copy-start.3
  74.0 0.9 %copy-done.3 = f32[256,256]{1,0:T(8,128)S(1)} copy-done((f32[256,256]{1,0:T(8,128)S(1)}, f32[256,256]{1,0:T(8,128)}, u32[]{:S(2)}) %copy-start.3) | copy-done | bytes 262168
  75.0 0.0 copy-start.4
  75.0 0.9 %copy-done.4 = f32[256,256]{1,0:T(8,128)S(1)} copy-done((f32[256,256]{1,0:T(8,128)S(1)}, f32[256,256]{1,0:T(8,128)}, u32[]{:S(2)}) %copy-start.4) | copy-done | bytes 262168
  75.9 1.4 %finish.1 = (f32[256,256]{1,0:T(8,128)}, f32[256,256]{1,0:T(8,128)}, f32[256,256]{1,0:T(8,128)}, f32[256,256]{1,0:T(8,128)}, f32[256,256]{1,0:T(8,128)}) custom-call(f32[256,512]{1,0:T(8,128)S(1)} %copy-done, f32[256,256]{1,0:T(8,128)S(1)} %copy-done.1, f32[256,256]{1,0:T(8,128)S(1)} %copy-done.2, f32[256,256]{1,0:T(8,128)S(1)} %copy-done.3, ...), custom_call_target="tpu_custom_call" | custom-call | tf_op jit(solution)/shard_map/finish/pallas_call | solution.py:367
Async XLA Ops:
  71.1 1.0 %copy-start = (f32[256,512]{1,0:T(8,128)S(1)}, f32[256,512]{1,0:T(8,128)}, u32[]{:S(2)}) copy-start(f32[256,512]{1,0:T(8,128)} %get-tuple-element.15.w) | copy-start | bytes 1572868
  72.1 0.9 %copy-start.1 = (f32[256,256]{1,0:T(8,128)S(1)}, f32[256,256]{1,0:T(8,128)}, u32[]{:S(2)}) copy-start(f32[256,256]{1,0:T(8,128)} %get-tuple-element.16.total_one) | copy-start | bytes 786436
  73.1 0.9 %copy-start.2 = (f32[256,256]{1,0:T(8,128)S(1)}, f32[256,256]{1,0:T(8,128)}, u32[]{:S(2)}) copy-start(f32[256,256]{1,0:T(8,128)} %get-tuple-element.17.mixed) | copy-start | bytes 786436
  74.0 0.9 %copy-start.3 = (f32[256,256]{1,0:T(8,128)S(1)}, f32[256,256]{1,0:T(8,128)}, u32[]{:S(2)}) copy-start(f32[256,256]{1,0:T(8,128)} %get-tuple-element.18.rest_two) | copy-start | bytes 786436
  75.0 0.9 %copy-start.4 = (f32[256,256]{1,0:T(8,128)S(1)}, f32[256,256]{1,0:T(8,128)}, u32[]{:S(2)}) copy-start(f32[256,256]{1,0:T(8,128)} %get-tuple-element.19.par) | copy-start | bytes 786436

commit v3 on v2

v3 whole, which is shorter than its diff:
```python
import functools

import jax
import jax.numpy as jnp
from jax import lax
from jax.experimental import pallas as pl
from jax.experimental.pallas import tpu as pltpu
from jax.sharding import PartitionSpec as P

MESH = pl.DeviceIdType.MESH
SIDE = 4
CORES = 2
POSITIONS = 4
PAIRS = tuple((i, k) for i in range(POSITIONS) for k in range(i, POSITIONS))
NP = len(PAIRS)
BLOCKS = 32
PARTS = 2
GROUPS = ((0, 2), (2, 2), (4, 2), (6, 2), (8, 2))
NEAR = BLOCKS // 2 + 1


def locate(a, b):
    d = jnp.bitwise_and(b - a + BLOCKS, BLOCKS - 1)
    swap = d >= NEAR
    return jnp.where(swap, b, a), jnp.where(swap, BLOCKS - d, d), swap


def parts(v):
    high = v.astype(jnp.bfloat16)
    return high, (v - high.astype(jnp.float32)).astype(jnp.bfloat16)


def mul(a, b, ca=1, cb=0):
    dims = (((ca,), (cb,)), ((), ()))
    dot = functools.partial(lax.dot_general, dimension_numbers=dims, preferred_element_type=jnp.float32)
    return dot(a[0], b[0]) + (dot(a[0], b[1]) + dot(a[1], b[0]))


def place(row):
    return row // (SIDE * CORES), lax.rem(row // CORES, SIDE), lax.rem(row, CORES)


def exchange_kernel(
    structure, root, panel_one, panel_two, inverse_one, parent, inverse_two,
    own_w, diag_one, mixed, rest_two, par,
    zed, loaded, u_all, u_high, u_low, w, table, rows,
    ag_00, ag_01, ag_10, ag_11, main_out, main_in, own_in,
    root_sem, load_sem, pan_send, pan_recv, pan_fsend, pan_frecv,
    ring_send, ring_recv, fwd_send, fwd_recv, core_send, core_recv,
    main_send, main_recv, z_send, z_recv, zf_send, zf_recv,
):
    width = panel_one.shape[0]
    quarter = width // SIDE
    part = quarter // PARTS
    half = part // 2
    sn = lax.axis_index("sn")
    z = lax.axis_index("blk")
    x, y, c = place(sn)
    ag = ((ag_00, ag_01), (ag_10, ag_11))

    def at(xx, yy, cc):
        return (xx * SIDE + yy) * CORES + cc

    def turn(v, o):
        return lax.rem(v + o, SIDE)

    x_dev = [(at(turn(x, o), y, c), z) for o in range(SIDE)]
    y_dev = [(at(x, turn(y, o), c), z) for o in range(SIDE)]
    z_dev = [(sn, turn(z, o)) for o in range(SIDE)]
    twin = (at(x, y, 1 - c), z)
    BELOW, ABOVE = 3, 1
    step = (1, 3)

    own_rows = [
        pltpu.make_async_copy(
            root.at[pl.ds(pl.multiple_of(z * quarter + r * 8, 8), 8), :], rows.at[pl.ds(r * 8, 8)], root_sem.at[r]
        )
        for r in range(quarter // 8)
    ]
    for cp in own_rows:
        cp.start()
    loads = [
        pltpu.make_async_copy(src, loaded.at[n], load_sem.at[n])
        for n, src in enumerate((panel_one, inverse_one, panel_two, inverse_two, parent))
    ]
    for cp in loads:
        cp.start()

    barrier = pltpu.get_barrier_semaphore()
    partners = x_dev[1:] + y_dev[1:] + [z_dev[1], z_dev[3], twin]
    for dev in partners:
        pl.semaphore_signal(barrier, inc=1, device_id=dev, device_id_type=MESH)
    pl.semaphore_wait(barrier, len(partners))

    sent = []

    def remote(src, dst, ssem, rsem, dev):
        return pltpu.make_async_remote_copy(
            src_ref=src, dst_ref=dst, send_sem=ssem, recv_sem=rsem, device_id=dev, device_id_type=MESH
        )

    def push(*what):
        cp = remote(*what)
        cp.start()
        sent.append(cp)

    split = (NEAR + 1) // 2
    spans = ((0, split), (split, NEAR - split))
    axes = ((x, x_dev), (y, y_dev))

    def piece(v, h, o, s, core):
        return ag[v][h].at[pl.ds((turn(axes[h][0], o) * CORES + core) * NEAR + spans[s][0], spans[s][1])]

    def ring(v, h, e, s, o):
        return remote(piece(v, h, o, s, c), piece(v, h, o, s, c), ring_send.at[v, h, e, s], ring_recv.at[v, h, e, s], axes[h][1][step[e]])

    def forward(v, h, e, o):
        return remote(piece(v, h, o, e, c), piece(v, h, o, e, c), fwd_send.at[v, h, e], fwd_recv.at[v, h, e], axes[h][1][step[e]])

    def twins(v, h, o, s, core):
        return remote(piece(v, h, o, s, core), piece(v, h, o, s, core), core_send.at[v, h, o, s], core_recv.at[v, h, o, s], twin)

    def go(cp):
        cp.start()
        sent.append(cp)

    def reblock(v, h):
        base = (axes[h][0] * CORES + c) * NEAR
        top = v * part + h * half

        def one(d, carry):
            col = pl.multiple_of(lax.rem(sn + d, BLOCKS) * width, width)
            ag[v][h][base + d] = rows[top:top + half, pl.ds(col, width)]
            return carry

        lax.fori_loop(0, NEAR, one, 0)

    def own_out(v, h):
        for order in range(2):
            for e in range(2):
                go(ring(v, h, e, (order, 1 - order)[e], 0))
        for s in range(2):
            go(twins(v, h, 0, s, c))

    def first_in(v, h):
        for e in range(2):
            o = (BELOW, ABOVE)[e]
            ring(v, h, e, e, o).wait_recv()
            go(forward(v, h, e, o))
            go(twins(v, h, o, e, c))

    def second_in(v, h):
        for e in range(2):
            o = (BELOW, ABOVE)[e]
            ring(v, h, e, 1 - e, o).wait_recv()
            go(twins(v, h, o, 1 - e, c))

    def far_in(v, h):
        for e in range(2):
            forward(v, h, e, 2).wait_recv()
            go(twins(v, h, 2, e, c))

    def twins_in(v, h):
        for o in (0, BELOW, ABOVE, 2):
            for s in range(2):
                twins(v, h, o, s, 1 - c).wait_recv()

    routes = ((y, y_dev), (x, x_dev))

    def listed(v, h, o, g):
        lo, n = GROUPS[g]
        return remote(
            main_out.at[v, h, o - 1, pl.ds(lo, n)], main_in.at[v, h, o - 1, pl.ds(lo, n)],
            main_send.at[v, h, o - 1, g], main_recv.at[v, h, o - 1, g], routes[h][1][o],
        )

    def listed_out(v, g):
        lo, n = GROUPS[g]
        for o in (2, 1, 3):
            for h in range(2):
                for p in range(lo, lo + n):
                    main_out[v, h, o - 1, p] = ag[v][h][table[h * SIDE + o, p]]
                listed(v, h, o, g).start()
        for h in range(2):
            for p in range(lo, lo + n):
                own_in[v, h, p] = ag[v][h][table[h * SIDE, p]]

    def listed_sent(v, g):
        for o in range(1, SIDE):
            for h in range(2):
                listed(v, h, o, g).wait_send()

    def zpart(v, o, lo, n):
        return zed.at[pl.ds((v * SIDE + turn(z, o)) * NP + lo, n)]

    def z_copy(v, o, e, g):
        lo, n = GROUPS[g]
        return remote(zpart(v, o, lo, n), zpart(v, o, lo, n), z_send.at[v, e, g], z_recv.at[v, e, g], z_dev[step[e]])

    def z_forward(v, o, e, g):
        lo, n = GROUPS[g]
        return remote(
            zpart(v, o, lo + e * (n // 2), n // 2), zpart(v, o, lo + e * (n // 2), n // 2),
            zf_send.at[v, e, g], zf_recv.at[v, e, g], z_dev[step[e]],
        )

    def listed_in(v, g):
        lo, n = GROUPS[g]
        for h in range(2):
            pos = routes[h][0]
            for o in range(1, SIDE):
                listed(v, h, o, g).wait_recv()
            for p in range(lo, lo + n):
                who = table[h * SIDE, NP + p]
                value = own_in[v, h, p]
                for o in range(1, SIDE):
                    value = jnp.where(who == turn(pos, SIDE - o), main_in[v, h, o - 1, p], value)
                zed[(v * SIDE + z) * NP + p, h * half:(h + 1) * half] = value
        for e in range(2):
            go(z_copy(v, 0, e, g))

    def hand_on(v, g):
        for e in range(2):
            o = (BELOW, ABOVE)[e]
            z_copy(v, o, e, g).wait_recv()
            go(z_forward(v, o, e, g))

    def arrive(v, g):
        for e in range(2):
            z_forward(v, 2, e, g).wait_recv()

    def u_part(o, n):
        return u_all.at[turn(z, o), n]

    def u_copy(o, e, n):
        return remote(u_part(o, n), u_part(o, n), pan_send.at[e, n], pan_recv.at[e, n], z_dev[step[e]])

    def u_forward(o, e):
        return remote(u_part(o, e), u_part(o, e), pan_fsend.at[e], pan_frecv.at[e], z_dev[step[e]])

    def split_u(o):
        for n in range(2):
            at_k = turn(z, o)
            u_high[at_k, :, n * width:(n + 1) * width], u_low[at_k, :, n * width:(n + 1) * width] = parts(u_all[at_k, n])

    def fill(n, carry):
        o = lax.rem(n, SIDE)
        along_x = n // SIDE
        item = at(turn(x, o * along_x), turn(y, o * (1 - along_x)), c)
        for p, (i, k) in enumerate(PAIRS):
            row, dist, swap = locate(structure[i, item], structure[k, item])
            rx, ry, rc = place(row)
            table[n, p] = (jnp.where(along_x == 0, rx, ry) * CORES + rc) * NEAR + dist
            table[n, NP + p] = jnp.where(along_x == 0, ry, rx)
            table[n, 2 * NP + p] = swap.astype(jnp.int32)
        return carry

    def products(p):
        i, k = PAIRS[p]
        block = jnp.concatenate(
            [zed[(v * SIDE + q) * NP + p] for q in range(SIDE) for v in range(PARTS)], axis=0
        )
        flipped = block.T
        swap = table[0, 2 * NP + p] == 1
        direct = parts(jnp.where(swap, flipped, block))
        value = mul(direct, (u_high[k], u_low[k]))
        w[i] = value if i == 0 and k == 0 else w[i] + value
        if i != k:
            value = mul(parts(jnp.where(swap, block, flipped)), (u_high[i], u_low[i]))
            w[k] = value if i == 0 else w[k] + value
        if k == POSITIONS - 1:
            one = (u_high[i, :, :width], u_low[i, :, :width])
            two = (u_high[i, :, width:], u_low[i, :, width:])
            w_one, w_two = parts(w[i, :, :width]), parts(w[i, :, width:])
            diag_one[...] += mul(one, w_one, 0, 0)
            cross = mul(two, w_one, 0, 0)
            mixed[...] = cross if i == 0 else mixed[...] + cross
            rest_two[...] += mul(two, w_two, 0, 0)

    count = len(GROUPS)
    for cp in own_rows[:part // 8]:
        cp.wait()
    for h in range(2):
        reblock(0, h)
        own_out(0, h)
    for cp in loads:
        cp.wait()
    inv_one, inv_two = parts(loaded[1]), parts(loaded[3])
    u_all[z, 0] = mul(parts(loaded[0]), inv_one)
    u_all[z, 1] = mul(parts(loaded[2]), inv_two)
    for order in range(2):
        for e in range(2):
            go(u_copy(0, e, (order, 1 - order)[e]))
    for cp in own_rows[part // 8:]:
        cp.wait()
    for h in range(2):
        reblock(1, h)
    lax.fori_loop(0, 2 * SIDE, fill, 0)
    for h in range(2):
        first_in(0, h)
    for h in range(2):
        second_in(0, h)
    for h in range(2):
        own_out(1, h)
    for e in range(2):
        o = (BELOW, ABOVE)[e]
        u_copy(o, e, e).wait_recv()
        go(u_forward(o, e))
    for h in range(2):
        far_in(0, h)
    par[...] = mul(parts(loaded[4]), inv_two)
    for h in range(2):
        twins_in(0, h)
    listed_out(0, 0)
    listed_out(0, 1)
    diag_one[...] = mul(inv_one, inv_one, 0, 0)
    rest_two[...] = mul(inv_two, inv_two, 0, 0)
    for h in range(2):
        first_in(1, h)
    listed_sent(0, 0)
    listed_out(0, 2)
    listed_in(0, 0)
    for h in range(2):
        second_in(1, h)
    listed_sent(0, 1)
    listed_out(0, 3)
    listed_in(0, 1)
    listed_sent(0, 2)
    listed_out(0, 4)
    split_u(0)
    for h in range(2):
        far_in(1, h)
    listed_in(0, 2)
    for h in range(2):
        twins_in(1, h)
    listed_out(1, 0)
    listed_out(1, 1)
    hand_on(0, 0)
    listed_in(0, 3)
    listed_in(0, 4)
    hand_on(0, 1)
    for e in range(2):
        u_copy((BELOW, ABOVE)[e], e, 1 - e).wait_recv()
        u_forward(2, e).wait_recv()
    for t in range(count + 2):
        if t + 2 < count:
            listed_sent(1, t)
            listed_out(1, t + 2)
            hand_on(0, t + 2)
        if t < count:
            listed_in(1, t)
        if t == 0:
            split_u(1)
            split_u(2)
        if 1 <= t <= count:
            hand_on(1, t - 1)
        if t >= 2:
            arrive(0, t - 2)
            arrive(1, t - 2)
            lo, n = GROUPS[t - 2]
            if t == 2:
                split_u(3)
            for p in range(lo, lo + n):
                products(p)
    for v, g in ((0, 3), (0, 4), (1, 3), (1, 4)):
        listed_sent(v, g)
    own_w[...] = w[z]
    for cp in sent:
        cp.wait_send()


def exchange(structure, root, panel_one, panel_two, inverse_one, parent, inverse_two):
    width = panel_one.shape[0]
    quarter = width // SIDE
    part = quarter // PARTS
    half = part // 2
    f32 = jnp.float32
    dma = pltpu.SemaphoreType.DMA
    hbm = pl.BlockSpec(memory_space=pltpu.HBM)
    vmem = pl.BlockSpec(memory_space=pltpu.VMEM)
    groups = len(GROUPS)
    square = jax.ShapeDtypeStruct((width, width), f32)
    gathered = pltpu.VMEM((SIDE * CORES * NEAR, half, width), f32)
    return pl.pallas_call(
        exchange_kernel,
        out_shape=(jax.ShapeDtypeStruct((width, 2 * width), f32),) + (square,) * 4,
        in_specs=[pl.BlockSpec(memory_space=pltpu.SMEM)] + [hbm] * 6,
        out_specs=(vmem,) * 5,
        scratch_shapes=[
            pltpu.VMEM((PARTS * SIDE * NP, part, width), f32),
            pltpu.VMEM((5, width, width), f32),
            pltpu.VMEM((POSITIONS, 2, width, width), f32),
            pltpu.VMEM((POSITIONS, width, 2 * width), jnp.bfloat16),
            pltpu.VMEM((POSITIONS, width, 2 * width), jnp.bfloat16),
            pltpu.VMEM((POSITIONS, width, 2 * width), f32),
            pltpu.SMEM((2 * SIDE, 3 * NP), jnp.int32),
            pltpu.VMEM((quarter, root.shape[1]), f32),
            gathered, gathered, gathered, gathered,
            pltpu.VMEM((PARTS, 2, SIDE - 1, NP, half, width), f32),
            pltpu.VMEM((PARTS, 2, SIDE - 1, NP, half, width), f32),
            pltpu.VMEM((PARTS, 2, NP, half, width), f32),
            dma((quarter // 8,)),
            dma((5,)),
            dma((2, 2)), dma((2, 2)), dma((2,)), dma((2,)),
            dma((PARTS, 2, 2, 2)), dma((PARTS, 2, 2, 2)), dma((PARTS, 2, 2)), dma((PARTS, 2, 2)),
            dma((PARTS, 2, SIDE, 2)), dma((PARTS, 2, SIDE, 2)),
            dma((PARTS, 2, SIDE - 1, groups)), dma((PARTS, 2, SIDE - 1, groups)),
            dma((PARTS, 2, groups)), dma((PARTS, 2, groups)), dma((PARTS, 2, groups)), dma((PARTS, 2, groups)),
        ],
        compiler_params=pltpu.CompilerParams(
            collective_id=0, has_side_effects=True, vmem_limit_bytes=57 * 2**20
        ),
        name="exchange",
    )(structure, root, panel_one, panel_two, inverse_one, parent, inverse_two)


def finish_kernel(w, total_one, mixed, rest_two, par, diag_one, off_one, diag_two, par_two, root_two):
    width = par.shape[0]
    u_par = parts(par[...])
    w_one = w[:, :width]
    diag_one[...] = total_one[...]
    off_one[...] = -w_one
    root_two[...] = mul(parts(w_one), u_par) - w[:, width:]
    cross = mixed[...]
    p_two = cross.T - mul(parts(total_one[...]), u_par)
    par_two[...] = p_two
    diag_two[...] = rest_two[...] - mul(parts(cross), u_par) - mul(u_par, parts(p_two), 0, 0)


def finish(*args):
    vmem = pl.BlockSpec(memory_space=pltpu.VMEM)
    return pl.pallas_call(
        finish_kernel,
        out_shape=(jax.ShapeDtypeStruct(args[-1].shape, jnp.float32),) * 5,
        in_specs=[vmem] * 5,
        out_specs=(vmem,) * 5,
        compiler_params=pltpu.CompilerParams(vmem_limit_bytes=60 * 2**20),
        name="finish",
    )(*args)


def per_device(root_inverse, structure, panel_one, inverse_one, parent_two, panel_two, inverse_two):
    sums = exchange(
        structure.T, root_inverse, panel_one[0], panel_two[0], inverse_one[0], parent_two[0], inverse_two[0]
    )
    return tuple(out[None] for out in finish(*sums))


def solution(mesh):
    return jax.shard_map(
        per_device,
        mesh=mesh,
        in_specs=(
            P("sn", None),
            P(),
            P("sn", "blk", None),
            P("sn", None, None),
            P("sn", None, None),
            P("sn", "blk", None),
            P("sn", None, None),
        ),
        out_specs=(
            P("sn", None, None),
            P("sn", "blk", None),
            P("sn", None, None),
            P("sn", None, None),
            P("sn", "blk", None),
        ),
        check_vma=False,
    )
```

time: 78 us -> 69.8 us (0.89)
  local copies, waits for them, and re-layouts: 6.2 us -> 0 us
  Pallas kernels: 70.5 us -> 69 us
    unnamed x11 -> x0, local copies, waits for them, and re-layouts: 6.2 us -> none
    pallas_call x1, Pallas kernels: 69.1 us -> 66.2 us  [exchange(): pl.pallas_call(exchange_kernel, out_shape=(jax.ShapeDtypeStruct((width, 2...]
    pallas_call x1, Pallas kernels: 1.44 us -> 2.8 us  [finish(): pl.pallas_call(finish_kernel, out_shape=(jax.ShapeDtypeStruct(args[-1].sh...]
where the time goes in v3:
time: 69.8 us; the launch traced here: 69.6 us
  Pallas kernels  69 us (99%)
    pallas_call x1, Pallas kernels, exchange(): pl.pallas_call(exchange_kernel, out_shape=(jax.ShapeDtypeStruct((width, 2...  66.2 us
    pallas_call x1, Pallas kernels, finish(): pl.pallas_call(finish_kernel, out_shape=(jax.ShapeDtypeStruct(args[-1].sh...  2.8 us

profile of v3, /device:TPU:0, one launch (start us, length us, event | category | flops | bytes accessed | tf_op | source)
XLA Modules:
  0.0 69.6 jit_solution(6151050203940208973)
XLA Ops:
  0.6 66.2 %exchange.1 = (f32[256,512]{1,0:T(8,128)}, f32[256,256]{1,0:T(8,128)}, f32[256,256]{1,0:T(8,128)}, f32[256,256]{1,0:T(8,128)}, f32[256,256]{1,0:T(8,128)}) custom-call(s32[4,32]{1,0:T(4,128)} %bitcast.16, f32[256,8192]{1,0:T(8,128)} %root.1, f32[256,256]{1,0:T(8,128)} %bitcast.11, f32[256,256]{1,0:T(8,128)} %bitcast.12, f32[256,256]{1,0:T(8,128)} %bitcast.13, ...), custom_call_target="tpu_custom_call" | custom-call | tf_op jit(solution)/shard_map/exchange/pallas_call | solution.py:384
  66.8 2.8 %finish.1 = (f32[256,256]{1,0:T(8,128)}, f32[256,256]{1,0:T(8,128)}, f32[256,256]{1,0:T(8,128)}, f32[256,256]{1,0:T(8,128)}, f32[256,256]{1,0:T(8,128)}) custom-call(f32[256,512]{1,0:T(8,128)} %get-tuple-element.15.w, f32[256,256]{1,0:T(8,128)} %get-tuple-element.16.total_one, f32[256,256]{1,0:T(8,128)} %get-tuple-element.17.mixed, ...), custom_call_target="tpu_custom_call" | custom-call | tf_op jit(solution)/shard_map/finish/pallas_call | solution.py:432

commit v4 on v3

--- a/solution.py
+++ b/solution.py
@@ -15,8 +15,18 @@
 NP = len(PAIRS)
 BLOCKS = 32
 PARTS = 2
-GROUPS = ((0, 2), (2, 2), (4, 2), (6, 2), (8, 2))
+GROUPS = ((0, 4), (4, 4), (8, 2))
 NEAR = BLOCKS // 2 + 1
+
+
+SEQUENCE = (
+    ("F", 0), ("S", 0), ("O", 1), ("U",), ("R", 0), ("Q",), ("T", 0), ("L", 0, 0),
+    ("L", 0, 1), ("L", 0, 2), ("D",), ("F", 1), ("I", 0, 0), ("S", 1), ("I", 0, 1), ("H", 0, 0),
+    ("R", 1), ("I", 0, 2), ("H", 0, 1), ("X", 0), ("T", 1), ("L", 1, 0), ("L", 1, 1), ("L", 1, 2),
+    ("H", 0, 2), ("V",), ("I", 1, 0), ("X", 1), ("X", 2), ("I", 1, 1), ("H", 1, 0), ("I", 1, 2),
+    ("H", 1, 1), ("A", 0, 0), ("A", 1, 0), ("X", 3), ("P", 0), ("H", 1, 2), ("A", 0, 1), ("A", 1, 1),
+    ("P", 1), ("A", 0, 2), ("A", 1, 2), ("P", 2),
+)
 
 
 def locate(a, b):
@@ -32,8 +42,9 @@
 
 def mul(a, b, ca=1, cb=0):
     dims = (((ca,), (cb,)), ((), ()))
-    dot = functools.partial(lax.dot_general, dimension_numbers=dims, preferred_element_type=jnp.float32)
-    return dot(a[0], b[0]) + (dot(a[0], b[1]) + dot(a[1], b[0]))
+    left = jnp.concatenate([a[0], a[0], a[1]], axis=ca)
+    right = jnp.concatenate([b[0], b[1], b[0]], axis=cb)
+    return lax.dot_general(left, right, dimension_numbers=dims, preferred_element_type=jnp.float32)
 
 
 def place(row):
@@ -277,7 +288,6 @@
             mixed[...] = cross if i == 0 else mixed[...] + cross
             rest_two[...] += mul(two, w_two, 0, 0)
 
-    count = len(GROUPS)
     for cp in own_rows[:part // 8]:
         cp.wait()
     for h in range(2):
@@ -296,74 +306,47 @@
     for h in range(2):
         reblock(1, h)
     lax.fori_loop(0, 2 * SIDE, fill, 0)
-    for h in range(2):
-        first_in(0, h)
-    for h in range(2):
-        second_in(0, h)
-    for h in range(2):
-        own_out(1, h)
-    for e in range(2):
-        o = (BELOW, ABOVE)[e]
-        u_copy(o, e, e).wait_recv()
-        go(u_forward(o, e))
-    for h in range(2):
-        far_in(0, h)
-    par[...] = mul(parts(loaded[4]), inv_two)
-    for h in range(2):
-        twins_in(0, h)
-    listed_out(0, 0)
-    listed_out(0, 1)
-    diag_one[...] = mul(inv_one, inv_one, 0, 0)
-    rest_two[...] = mul(inv_two, inv_two, 0, 0)
-    for h in range(2):
-        first_in(1, h)
-    listed_sent(0, 0)
-    listed_out(0, 2)
-    listed_in(0, 0)
-    for h in range(2):
-        second_in(1, h)
-    listed_sent(0, 1)
-    listed_out(0, 3)
-    listed_in(0, 1)
-    listed_sent(0, 2)
-    listed_out(0, 4)
-    split_u(0)
-    for h in range(2):
-        far_in(1, h)
-    listed_in(0, 2)
-    for h in range(2):
-        twins_in(1, h)
-    listed_out(1, 0)
-    listed_out(1, 1)
-    hand_on(0, 0)
-    listed_in(0, 3)
-    listed_in(0, 4)
-    hand_on(0, 1)
-    for e in range(2):
-        u_copy((BELOW, ABOVE)[e], e, 1 - e).wait_recv()
-        u_forward(2, e).wait_recv()
-    for t in range(count + 2):
-        if t + 2 < count:
-            listed_sent(1, t)
-            listed_out(1, t + 2)
-            hand_on(0, t + 2)
-        if t < count:
-            listed_in(1, t)
-        if t == 0:
-            split_u(1)
-            split_u(2)
-        if 1 <= t <= count:
-            hand_on(1, t - 1)
-        if t >= 2:
-            arrive(0, t - 2)
-            arrive(1, t - 2)
-            lo, n = GROUPS[t - 2]
-            if t == 2:
-                split_u(3)
-            for p in range(lo, lo + n):
-                products(p)
-    for v, g in ((0, 3), (0, 4), (1, 3), (1, 4)):
-        listed_sent(v, g)
+    def both(f):
+        def run(v):
+            for h in range(2):
+                f(v, h)
+
+        return run
+
+    def u_on():
+        for e in range(2):
+            o = (BELOW, ABOVE)[e]
+            u_copy(o, e, e).wait_recv()
+            go(u_forward(o, e))
+
+    def u_in():
+        for e in range(2):
+            u_copy((BELOW, ABOVE)[e], e, 1 - e).wait_recv()
+            u_forward(2, e).wait_recv()
+
+    def squares():
+        diag_one[...] = mul(inv_one, inv_one, 0, 0)
+        rest_two[...] = mul(inv_two, inv_two, 0, 0)
+
+    def u_parent():
+        par[...] = mul(parts(loaded[4]), inv_two)
+
+    def multiply(g):
+        lo, n = GROUPS[g]
+        for p in range(lo, lo + n):
+            products(p)
+
+    steps = {
+        "O": both(own_out), "F": both(first_in), "S": both(second_in), "R": both(far_in), "T": both(twins_in),
+        "L": listed_out, "K": listed_sent, "I": listed_in, "H": hand_on, "A": arrive, "P": multiply,
+        "U": u_on, "V": u_in, "D": squares, "Q": u_parent, "X": split_u,
+    }
+    for name, *at_what in SEQUENCE:
+        steps[name](*at_what)
+    for v in range(PARTS):
+        for g in range(len(GROUPS)):
+            if ("K", v, g) not in SEQUENCE:
+                listed_sent(v, g)
     own_w[...] = w[z]
     for cp in sent:
         cp.wait_send()

time: 69.8 us -> 67.7 us (0.970)
  Pallas kernels: 69 us -> 66.9 us
    pallas_call x1, Pallas kernels: 66.2 us -> 64.1 us  [exchange(): pl.pallas_call(exchange_kernel, out_shape=(jax.ShapeDtypeStruct((width, 2...]
where the time goes in v4:
time: 67.7 us; the launch traced here: 67.6 us
  Pallas kernels  66.9 us (99%)
    pallas_call x1, Pallas kernels, exchange(): pl.pallas_call(exchange_kernel, out_shape=(jax.ShapeDtypeStruct((width, 2...  64.1 us
    pallas_call x1, Pallas kernels, finish(): pl.pallas_call(finish_kernel, out_shape=(jax.ShapeDtypeStruct(args[-1].sh...  2.79 us

profile of v4, /device:TPU:0, one launch (start us, length us, event | category | flops | bytes accessed | tf_op | source)
XLA Modules:
  0.0 67.6 jit_solution(5131187939574724269)
XLA Ops:
  0.6 64.1 %exchange.1 = (f32[256,512]{1,0:T(8,128)}, f32[256,256]{1,0:T(8,128)}, f32[256,256]{1,0:T(8,128)}, f32[256,256]{1,0:T(8,128)}, f32[256,256]{1,0:T(8,128)}) custom-call(s32[4,32]{1,0:T(4,128)} %bitcast.16, f32[256,8192]{1,0:T(8,128)} %root.1, f32[256,256]{1,0:T(8,128)} %bitcast.11, f32[256,256]{1,0:T(8,128)} %bitcast.12, f32[256,256]{1,0:T(8,128)} %bitcast.13, ...), custom_call_target="tpu_custom_call" | custom-call | tf_op jit(solution)/shard_map/exchange/pallas_call | solution.py:367
  64.8 2.8 %finish.1 = (f32[256,256]{1,0:T(8,128)}, f32[256,256]{1,0:T(8,128)}, f32[256,256]{1,0:T(8,128)}, f32[256,256]{1,0:T(8,128)}, f32[256,256]{1,0:T(8,128)}) custom-call(f32[256,512]{1,0:T(8,128)} %get-tuple-element.15.w, f32[256,256]{1,0:T(8,128)} %get-tuple-element.16.total_one, f32[256,256]{1,0:T(8,128)} %get-tuple-element.17.mixed, ...), custom_call_target="tpu_custom_call" | custom-call | tf_op jit(solution)/shard_map/finish/pallas_call | solution.py:415

commit v5 on v4

--- a/solution.py
+++ b/solution.py
@@ -15,17 +15,20 @@
 NP = len(PAIRS)
 BLOCKS = 32
 PARTS = 2
-GROUPS = ((0, 4), (4, 4), (8, 2))
+GROUPS = ((0, 2), (2, 2), (4, 2), (6, 2), (8, 2))
 NEAR = BLOCKS // 2 + 1
 
 
 SEQUENCE = (
     ("F", 0), ("S", 0), ("O", 1), ("U",), ("R", 0), ("Q",), ("T", 0), ("L", 0, 0),
-    ("L", 0, 1), ("L", 0, 2), ("D",), ("F", 1), ("I", 0, 0), ("S", 1), ("I", 0, 1), ("H", 0, 0),
-    ("R", 1), ("I", 0, 2), ("H", 0, 1), ("X", 0), ("T", 1), ("L", 1, 0), ("L", 1, 1), ("L", 1, 2),
-    ("H", 0, 2), ("V",), ("I", 1, 0), ("X", 1), ("X", 2), ("I", 1, 1), ("H", 1, 0), ("I", 1, 2),
-    ("H", 1, 1), ("A", 0, 0), ("A", 1, 0), ("X", 3), ("P", 0), ("H", 1, 2), ("A", 0, 1), ("A", 1, 1),
-    ("P", 1), ("A", 0, 2), ("A", 1, 2), ("P", 2),
+    ("L", 0, 1), ("K", 0, 0), ("L", 0, 2), ("D",), ("F", 1), ("I", 0, 0), ("K", 0, 1), ("L", 0, 3),
+    ("I", 0, 1), ("H", 0, 0), ("S", 1), ("K", 0, 2), ("L", 0, 4), ("I", 0, 2), ("H", 0, 1), ("R", 1),
+    ("I", 0, 3), ("H", 0, 2), ("T", 1), ("L", 1, 0), ("L", 1, 1), ("I", 0, 4), ("H", 0, 3), ("V",),
+    ("H", 0, 4), ("K", 1, 0), ("L", 1, 2), ("X", 0), ("I", 1, 0), ("K", 1, 1), ("L", 1, 3), ("X", 1),
+    ("I", 1, 1), ("H", 1, 0), ("K", 1, 2), ("L", 1, 4), ("X", 2), ("I", 1, 2), ("H", 1, 1), ("X", 3),
+    ("I", 1, 3), ("H", 1, 2), ("A", 0, 0), ("A", 1, 0), ("P", 0), ("I", 1, 4), ("H", 1, 3), ("A", 0, 1),
+    ("A", 1, 1), ("P", 1), ("H", 1, 4), ("A", 0, 2), ("A", 1, 2), ("P", 2), ("A", 0, 3), ("A", 1, 3),
+    ("P", 3), ("A", 0, 4), ("A", 1, 4), ("P", 4),
 )
 
 
@@ -82,6 +85,10 @@
     BELOW, ABOVE = 3, 1
     step = (1, 3)
 
+    barrier = pltpu.get_barrier_semaphore()
+    partners = x_dev[1:] + y_dev[1:] + [z_dev[1], z_dev[3], twin]
+    for dev in partners:
+        pl.semaphore_signal(barrier, inc=1, device_id=dev, device_id_type=MESH)
     own_rows = [
         pltpu.make_async_copy(
             root.at[pl.ds(pl.multiple_of(z * quarter + r * 8, 8), 8), :], rows.at[pl.ds(r * 8, 8)], root_sem.at[r]
@@ -96,11 +103,6 @@
     ]
     for cp in loads:
         cp.start()
-
-    barrier = pltpu.get_barrier_semaphore()
-    partners = x_dev[1:] + y_dev[1:] + [z_dev[1], z_dev[3], twin]
-    for dev in partners:
-        pl.semaphore_signal(barrier, inc=1, device_id=dev, device_id_type=MESH)
     pl.semaphore_wait(barrier, len(partners))
 
     sent = []

time: 67.7 us -> 67.4 us (level)
  no operation moved by 1% of the time
where the time goes in v5:
time: 67.4 us; the launch traced here: 67.3 us
  Pallas kernels  66.6 us (99%)
    pallas_call x1, Pallas kernels, exchange(): pl.pallas_call(exchange_kernel, out_shape=(jax.ShapeDtypeStruct((width, 2...  63.9 us
    pallas_call x1, Pallas kernels, finish(): pl.pallas_call(finish_kernel, out_shape=(jax.ShapeDtypeStruct(args[-1].sh...  2.79 us

profile of v5, /device:TPU:0, one launch (start us, length us, event | category | flops | bytes accessed | tf_op | source)
XLA Modules:
  0.0 67.3 jit_solution(12523954822515844451)
XLA Ops:
  0.6 63.9 %exchange.1 = (f32[256,512]{1,0:T(8,128)}, f32[256,256]{1,0:T(8,128)}, f32[256,256]{1,0:T(8,128)}, f32[256,256]{1,0:T(8,128)}, f32[256,256]{1,0:T(8,128)}) custom-call(s32[4,32]{1,0:T(4,128)} %bitcast.16, f32[256,8192]{1,0:T(8,128)} %root.1, f32[256,256]{1,0:T(8,128)} %bitcast.11, f32[256,256]{1,0:T(8,128)} %bitcast.12, f32[256,256]{1,0:T(8,128)} %bitcast.13, ...), custom_call_target="tpu_custom_call" | custom-call | tf_op jit(solution)/shard_map/exchange/pallas_call | solution.py:369
  64.5 2.8 %finish.1 = (f32[256,256]{1,0:T(8,128)}, f32[256,256]{1,0:T(8,128)}, f32[256,256]{1,0:T(8,128)}, f32[256,256]{1,0:T(8,128)}, f32[256,256]{1,0:T(8,128)}) custom-call(f32[256,512]{1,0:T(8,128)} %get-tuple-element.15.w, f32[256,256]{1,0:T(8,128)} %get-tuple-element.16.total_one, f32[256,256]{1,0:T(8,128)} %get-tuple-element.17.mixed, ...), custom_call_target="tpu_custom_call" | custom-call | tf_op jit(solution)/shard_map/finish/pallas_call | solution.py:417

commit v6 on v4

--- a/solution.py
+++ b/solution.py
@@ -15,6 +15,7 @@
 NP = len(PAIRS)
 BLOCKS = 32
 PARTS = 2
+DIRECT = ((1, 2),)
 GROUPS = ((0, 4), (4, 4), (8, 2))
 NEAR = BLOCKS // 2 + 1
 
@@ -98,7 +99,7 @@
         cp.start()
 
     barrier = pltpu.get_barrier_semaphore()
-    partners = x_dev[1:] + y_dev[1:] + [z_dev[1], z_dev[3], twin]
+    partners = x_dev[1:] + y_dev[1:] + z_dev[1:] + [twin]
     for dev in partners:
         pl.semaphore_signal(barrier, inc=1, device_id=dev, device_id_type=MESH)
     pl.semaphore_wait(barrier, len(partners))
@@ -207,6 +208,10 @@
     def z_copy(v, o, e, g):
         lo, n = GROUPS[g]
         return remote(zpart(v, o, lo, n), zpart(v, o, lo, n), z_send.at[v, e, g], z_recv.at[v, e, g], z_dev[step[e]])
+
+    def z_direct(v, o, g):
+        lo, n = GROUPS[g]
+        return remote(zpart(v, o, lo, n), zpart(v, o, lo, n), zf_send.at[v, 0, g], zf_recv.at[v, 0, g], z_dev[2])
 
     def z_forward(v, o, e, g):
         lo, n = GROUPS[g]
@@ -229,14 +234,20 @@
                 zed[(v * SIDE + z) * NP + p, h * half:(h + 1) * half] = value
         for e in range(2):
             go(z_copy(v, 0, e, g))
+        if (v, g) in DIRECT:
+            go(z_direct(v, 0, g))
 
     def hand_on(v, g):
         for e in range(2):
             o = (BELOW, ABOVE)[e]
             z_copy(v, o, e, g).wait_recv()
-            go(z_forward(v, o, e, g))
+            if (v, g) not in DIRECT:
+                go(z_forward(v, o, e, g))
 
     def arrive(v, g):
+        if (v, g) in DIRECT:
+            z_direct(v, 2, g).wait_recv()
+            return
         for e in range(2):
             z_forward(v, 2, e, g).wait_recv()
 

time: 67.7 us -> 67.7 us (level)
  no operation moved by 1% of the time
where the time goes in v6:
time: 67.7 us; the launch traced here: 67.5 us
  Pallas kernels  66.9 us (99%)
    pallas_call x1, Pallas kernels, exchange(): pl.pallas_call(exchange_kernel, out_shape=(jax.ShapeDtypeStruct((width, 2...  64.1 us
    pallas_call x1, Pallas kernels, finish(): pl.pallas_call(finish_kernel, out_shape=(jax.ShapeDtypeStruct(args[-1].sh...  2.79 us

profile of v6, /device:TPU:0, one launch (start us, length us, event | category | flops | bytes accessed | tf_op | source)
XLA Modules:
  0.0 67.5 jit_solution(941193567235592615)
XLA Ops:
  0.6 64.1 %exchange.1 = (f32[256,512]{1,0:T(8,128)}, f32[256,256]{1,0:T(8,128)}, f32[256,256]{1,0:T(8,128)}, f32[256,256]{1,0:T(8,128)}, f32[256,256]{1,0:T(8,128)}) custom-call(s32[4,32]{1,0:T(4,128)} %bitcast.16, f32[256,8192]{1,0:T(8,128)} %root.1, f32[256,256]{1,0:T(8,128)} %bitcast.11, f32[256,256]{1,0:T(8,128)} %bitcast.12, f32[256,256]{1,0:T(8,128)} %bitcast.13, ...), custom_call_target="tpu_custom_call" | custom-call | tf_op jit(solution)/shard_map/exchange/pallas_call | solution.py:378
  64.8 2.8 %finish.1 = (f32[256,256]{1,0:T(8,128)}, f32[256,256]{1,0:T(8,128)}, f32[256,256]{1,0:T(8,128)}, f32[256,256]{1,0:T(8,128)}, f32[256,256]{1,0:T(8,128)}) custom-call(f32[256,512]{1,0:T(8,128)} %get-tuple-element.15.w, f32[256,256]{1,0:T(8,128)} %get-tuple-element.16.total_one, f32[256,256]{1,0:T(8,128)} %get-tuple-element.17.mixed, ...), custom_call_target="tpu_custom_call" | custom-call | tf_op jit(solution)/shard_map/finish/pallas_call | solution.py:426
